TPU v7x, 32 devices: a whole 2x2x4 slice. The times are simulated.
32 devices in a mesh: dp: 4 (over z), expert: 8 (over y, x, core).
Axes of the slice: x: 2, y: 2, z: 4, core: 2. Of those that a mesh axis runs over, the one named last changes fastest.
Arguments:
- tokens: bfloat16 [4096, 2048], P(('dp', 'expert')), may hold values from -6 to 6
- norm1_gain: float32 [2048], replicated, may hold values from 0.25 to 1.75
- w_query: bfloat16 [2048, 4096], P('dp', 'expert'), may hold values from -0.125 to 0.125
- key_weight: bfloat16 [2048, 512], P('dp', 'expert'), may hold values from -0.125 to 0.125
- value_weight: bfloat16 [2048, 512], P('dp', 'expert'), may hold values from -0.125 to 0.125
- w_out: bfloat16 [4096, 2048], P('expert', 'dp'), may hold values from -1 to 1
- query_gain: float32 [128], replicated, may hold values from 0.25 to 1.75
- key_gain: float32 [128], replicated, may hold values from 0.25 to 1.75
- norm2_gain: float32 [2048], replicated, may hold values from 0.25 to 1.75
- w_router: bfloat16 [2048, 32], replicated, may hold values from -0.0625 to 0.0625
- w_gate: bfloat16 [32, 2048, 768], P(('dp', 'expert')), may hold values from -0.125 to 0.125
- w_up: bfloat16 [32, 2048, 768], P(('dp', 'expert')), may hold values from -0.125 to 0.125
- w_down: bfloat16 [32, 768, 2048], P(('dp', 'expert')), may hold values from -0.625 to 0.625
- routes: int32 [4096, 8], P(('dp', 'expert')), may hold values from 0 to 31, all different within a row; in each aligned block of 128 rows (0 to 127, 128 to 255, ...) at most 36 rows name the same one
- out_grad: bfloat16 [4096, 2048], P(('dp', 'expert')), may hold values from -6 to 6
Outputs:
- layer_out: bfloat16 [4096, 2048], P(('dp', 'expert'))
- grad_tokens: float32 [4096, 2048], P(('dp', 'expert'))
- grad_norm1_gain: float32 [2048], replicated
- grad_w_query: float32 [2048, 4096], P('dp', 'expert')
- grad_w_key: float32 [2048, 512], P('dp', 'expert')
- grad_w_value: float32 [2048, 512], P('dp', 'expert')
- grad_w_out: float32 [4096, 2048], P('expert', 'dp')
- grad_query_gain: float32 [128], replicated
- grad_key_gain: float32 [128], replicated
- grad_norm2_gain: float32 [2048], replicated
- grad_w_router: float32 [2048, 32], replicated
- grad_w_gate: float32 [32, 2048, 768], P(('dp', 'expert'))
- grad_w_up: float32 [32, 2048, 768], P(('dp', 'expert'))
- grad_w_down: float32 [32, 768, 2048], P(('dp', 'expert'))
Inputs may be any that keep to these rules, and one draw needn't show every extreme that they name: `routes`: each row names 8 different experts. In the rows of one device (aligned blocks of 128 rows) no expert is named by more than 36 rows, and in every draw some block names some expert exactly 36 times.
All inputs are finite; a program needn't handle non-finite values.
Results may differ from a plain program's by a relative error of at most 0.019.
Values may be sent and summed in bfloat16 or wider, within the bound.
A program may use at most 192 MiB of HBM per device.

v0:
```python
import jax
import jax.numpy as jnp
from jax import lax
from jax.sharding import PartitionSpec as P

SEQ_LEN = 1024


NORM_EPS = 1e-06
ROPE_THETA = 1000000.0


def swapped(block, axis, distance):
    count = lax.axis_size(axis)
    route = []
    for low in range(count):
        high = low | 1 << distance
        if high != low and high < count:
            route += [(low, high), (high, low)]
    return lax.ppermute(block, axis, route)


def rope_tables(count_of_rows, head_size, seq_len):
    position = (jnp.arange(count_of_rows) % seq_len).astype(jnp.float32)
    half_size = head_size // 2
    frequency = ROPE_THETA ** (-(jnp.arange(half_size).astype(jnp.float32) * 2.0) / head_size)
    angles = position[:, None] * frequency[None, :]
    angles = jnp.concatenate([angles, angles], axis=-1)
    return (jnp.cos(angles), jnp.sin(angles))


def rotate(value_tensor, cos_table, sine_table):
    half_size = value_tensor.shape[-1] // 2
    turned = jnp.concatenate(
        [-value_tensor[..., half_size:], value_tensor[..., :half_size]], axis=-1
    )
    return value_tensor * cos_table + turned * sine_table


def rotate_back(gradient, cos_table, sine_table):
    half_size = gradient.shape[-1] // 2
    turned = gradient * sine_table
    return gradient * cos_table + jnp.concatenate(
        [turned[..., half_size:], -turned[..., :half_size]], axis=-1
    )


def norm_forward(value_tensor, gain_vec):
    row_scale = lax.rsqrt(jnp.mean(value_tensor * value_tensor, axis=-1, keepdims=True) + NORM_EPS)
    return (value_tensor * row_scale * gain_vec, row_scale)


def norm_backward(gradient, value_tensor, row_scale, gain_vec):
    scaled = gradient * gain_vec
    inner = jnp.mean(scaled * value_tensor, axis=-1, keepdims=True)
    return row_scale * scaled - value_tensor * row_scale * row_scale * row_scale * inner


def move_rows(buffer):
    return lax.all_to_all(buffer, ("dp", "expert"), split_axis=0, concat_axis=0, tiled=True)


def local(
    tokens,
    norm1_gain,
    w_query,
    key_weight,
    value_weight,
    w_out,
    query_gain,
    key_gain,
    norm2_gain,
    w_router,
    w_gate,
    w_up,
    w_down,
    routes,
    out_grad,
):
    data_count = lax.axis_size("dp")
    group_count = lax.axis_size("expert")
    group_index = lax.axis_index("expert")
    local_rows = tokens.shape[0]
    model_width = tokens.shape[1]
    head_dim = query_gain.shape[0]
    heads_here = w_query.shape[1] // head_dim
    top_count = routes.shape[1]
    expert_total = data_count * group_count
    capacity = max(2, (local_rows * top_count * 9 + 8 * expert_total - 1) // (8 * expert_total))
    token_f = tokens.astype(jnp.float32)
    normed_f, first_scale = norm_forward(token_f, norm1_gain)
    normed_input = normed_f.astype(jnp.bfloat16)
    gathered = lax.all_gather(normed_input, "expert", axis=0, tiled=True)
    all_rows = gathered.shape[0]
    seq_len = min(SEQ_LEN, all_rows)
    q_cols, k_cols, v_cols, o_rows = (
        lax.all_gather(w_query, "dp", axis=0, tiled=True),
        lax.all_gather(key_weight, "dp", axis=0, tiled=True),
        lax.all_gather(value_weight, "dp", axis=0, tiled=True),
        lax.all_gather(w_out, "dp", axis=1, tiled=True),
    )
    heads_total = heads_here * group_count
    kv_heads = k_cols.shape[1] * group_count // head_dim
    sharing = heads_total // kv_heads // heads_here
    bit_count = sharing.bit_length() - 1
    k_head = k_cols
    v_head = v_cols
    for bit in range(bit_count):
        key_got, value_got = swapped((k_head, v_head), "expert", bit)
        upper_side = group_index // 2**bit % 2 == 1
        k_head = jnp.where(
            upper_side,
            jnp.concatenate([key_got, k_head], axis=1),
            jnp.concatenate([k_head, key_got], axis=1),
        )
        v_head = jnp.where(
            upper_side,
            jnp.concatenate([value_got, v_head], axis=1),
            jnp.concatenate([v_head, value_got], axis=1),
        )
    cos_table, sine_table = rope_tables(all_rows, head_dim, seq_len)
    cos_three = cos_table[:, None, :]
    sine_three = sine_table[:, None, :]
    query_raw = jnp.dot(gathered, q_cols, preferred_element_type=jnp.float32).reshape(
        all_rows, heads_here, head_dim
    )
    query_norm, query_scale = norm_forward(query_raw, query_gain)
    queries = rotate(query_norm, cos_three, sine_three).astype(jnp.bfloat16)
    key_raw = jnp.dot(gathered, k_head, preferred_element_type=jnp.float32)
    key_norm, key_scale = norm_forward(key_raw, key_gain)
    keys_low = rotate(key_norm, cos_table, sine_table).astype(jnp.bfloat16)
    values_low = jnp.dot(gathered, v_head, preferred_element_type=jnp.float32).astype(jnp.bfloat16)
    seq_count = all_rows // seq_len
    block_len = min(512, seq_len)
    block_count = seq_len // block_len
    score_scale = head_dim ** (-0.5)
    query_seq = queries.reshape(seq_count, seq_len, heads_here, head_dim)
    key_seq = keys_low.reshape(seq_count, seq_len, head_dim)
    value_seq = values_low.reshape(seq_count, seq_len, head_dim)

    def block_scores(block_id):
        start_row = block_id * block_len
        key_len = start_row + block_len
        query_part = query_seq[:, start_row:key_len]
        scores = (
            jnp.einsum(
                "nqhd,nkd->nhqk",
                query_part,
                key_seq[:, :key_len],
                preferred_element_type=jnp.float32,
            )
            * score_scale
        )
        query_pos = start_row + jnp.arange(block_len)
        allowed = jnp.arange(key_len)[None, :] <= query_pos[:, None]
        return (jnp.where(allowed, scores, -jnp.inf), query_part, key_len)

    outputs = []
    log_sums = []
    for block_id in range(block_count):
        scores, query_part, key_len = block_scores(block_id)
        row_max = jnp.max(scores, axis=-1, keepdims=True)
        exp_scores = jnp.exp(scores - row_max)
        totals = jnp.sum(exp_scores, axis=-1, keepdims=True)
        prob_low = (exp_scores / totals).astype(jnp.bfloat16)
        log_sums.append(row_max + jnp.log(totals))
        outputs.append(
            jnp.einsum(
                "nhqk,nkd->nqhd",
                prob_low,
                value_seq[:, :key_len],
                preferred_element_type=jnp.float32,
            ).astype(jnp.bfloat16)
        )
    attended = jnp.concatenate(outputs, axis=1).reshape(all_rows, heads_here * head_dim)
    branch = lax.psum_scatter(
        jnp.dot(attended, o_rows, preferred_element_type=jnp.float32),
        "expert",
        scatter_dimension=0,
        tiled=True,
    )
    hidden = token_f + branch
    second_f, second_scale = norm_forward(hidden, norm2_gain)
    second = second_f.astype(jnp.bfloat16)
    logits = jnp.dot(second, w_router, preferred_element_type=jnp.float32)
    expert_ids = jnp.arange(expert_total)
    one_hot = (routes[:, :, None] == expert_ids[None, None, :]).astype(jnp.float32)
    chosen = jnp.einsum("tke,te->tk", one_hot, logits, precision=lax.Precision.HIGHEST)
    gate_probs = jax.nn.softmax(chosen, axis=-1)
    entries = routes.reshape(-1)
    entry_hot = (entries[:, None] == expert_ids[None, :]).astype(jnp.int32)
    slot_rank = jnp.sum((jnp.cumsum(entry_hot, axis=0) - entry_hot) * entry_hot, axis=1)
    flat_place = entries * capacity + slot_rank
    token_of = jnp.arange(entries.shape[0]) // top_count
    send_rows = (
        jnp.zeros((expert_total * capacity, model_width), jnp.bfloat16)
        .at[flat_place]
        .set(second[token_of])
    )
    arrived = move_rows(send_rows.reshape(expert_total, capacity, model_width)).reshape(
        expert_total * capacity, model_width
    )
    gate_w = w_gate[0]
    up_w = w_up[0]
    down_w = w_down[0]
    gate_h = jnp.dot(arrived, gate_w, preferred_element_type=jnp.float32)
    up_h = jnp.dot(arrived, up_w, preferred_element_type=jnp.float32)
    sigmoid_h = jax.nn.sigmoid(gate_h)
    silu_h = gate_h * sigmoid_h
    active = (silu_h * up_h).astype(jnp.bfloat16)
    expert_out = jnp.dot(active, down_w, preferred_element_type=jnp.float32).astype(jnp.bfloat16)
    returned = move_rows(expert_out.reshape(expert_total, capacity, model_width)).reshape(
        expert_total * capacity, model_width
    )
    picked = returned[flat_place].reshape(local_rows, top_count, model_width).astype(jnp.float32)
    mixture = jnp.einsum("tk,tkd->td", gate_probs, picked, precision=lax.Precision.HIGHEST)
    output = (hidden + mixture).astype(jnp.bfloat16)
    grad_out = out_grad.astype(jnp.float32)
    grad_gate = jnp.sum(picked * grad_out[:, None, :], axis=-1)
    grad_slots = (
        (gate_probs[:, :, None] * grad_out[:, None, :])
        .astype(jnp.bfloat16)
        .reshape(-1, model_width)
    )
    send_grads = (
        jnp.zeros((expert_total * capacity, model_width), jnp.bfloat16)
        .at[flat_place]
        .set(grad_slots)
    )
    grad_arrived = move_rows(send_grads.reshape(expert_total, capacity, model_width)).reshape(
        expert_total * capacity, model_width
    )
    grad_active = jnp.einsum("rd,fd->rf", grad_arrived, down_w, preferred_element_type=jnp.float32)
    grad_gate_h = (grad_active * up_h * sigmoid_h * (1.0 + gate_h * (1.0 - sigmoid_h))).astype(
        jnp.bfloat16
    )
    grad_up_h = (grad_active * silu_h).astype(jnp.bfloat16)
    grad_down = jnp.einsum("rf,rd->fd", active, grad_arrived, preferred_element_type=jnp.float32)[
        None
    ]
    grad_gate_w = jnp.einsum("rd,rf->df", arrived, grad_gate_h, preferred_element_type=jnp.float32)[
        None
    ]
    grad_up_w = jnp.einsum("rd,rf->df", arrived, grad_up_h, preferred_element_type=jnp.float32)[
        None
    ]
    grad_rows = (
        jnp.einsum("rf,df->rd", grad_gate_h, gate_w, preferred_element_type=jnp.float32)
        + jnp.einsum("rf,df->rd", grad_up_h, up_w, preferred_element_type=jnp.float32)
    ).astype(jnp.bfloat16)
    grad_back = move_rows(grad_rows.reshape(expert_total, capacity, model_width)).reshape(
        expert_total * capacity, model_width
    )
    grad_second = jnp.sum(
        grad_back[flat_place].reshape(local_rows, top_count, model_width).astype(jnp.float32),
        axis=1,
    )
    grad_chosen = gate_probs * (grad_gate - jnp.sum(gate_probs * grad_gate, axis=-1, keepdims=True))
    grad_logits = jnp.einsum(
        "tke,tk->te", one_hot, grad_chosen, precision=lax.Precision.HIGHEST
    ).astype(jnp.bfloat16)
    grad_router = jnp.einsum("td,te->de", second, grad_logits, preferred_element_type=jnp.float32)
    grad_second = grad_second + jnp.einsum(
        "te,de->td", grad_logits, w_router, preferred_element_type=jnp.float32
    )
    grad_norm2 = jnp.sum(grad_second * hidden * second_scale, axis=0)
    grad_hidden = grad_out + norm_backward(grad_second, hidden, second_scale, norm2_gain)
    grad_branch = lax.all_gather(grad_hidden.astype(jnp.bfloat16), "expert", axis=0, tiled=True)
    grad_wout = jnp.einsum("th,td->hd", attended, grad_branch, preferred_element_type=jnp.float32)
    grad_attended = jnp.einsum(
        "td,hd->th", grad_branch, o_rows, preferred_element_type=jnp.float32
    ).astype(jnp.bfloat16)
    grad_att_seq = grad_attended.reshape(seq_count, seq_len, heads_here, head_dim)
    grad_queries = []
    grad_keys = jnp.zeros((seq_count, seq_len, head_dim), jnp.float32)
    grad_values = jnp.zeros((seq_count, seq_len, head_dim), jnp.float32)
    for block_id in range(block_count):
        scores, query_part, key_len = block_scores(block_id)
        prob_full = jnp.exp(scores - log_sums[block_id])
        prob_low = prob_full.astype(jnp.bfloat16)
        grad_part = grad_att_seq[:, block_id * block_len : key_len]
        key_part = key_seq[:, :key_len]
        grad_probs = jnp.einsum(
            "nqhd,nkd->nhqk", grad_part, value_seq[:, :key_len], preferred_element_type=jnp.float32
        )
        inner_sum = jnp.sum(prob_full * grad_probs, axis=-1, keepdims=True)
        grad_scores = (prob_full * (grad_probs - inner_sum) * score_scale).astype(jnp.bfloat16)
        grad_queries.append(
            jnp.einsum("nhqk,nkd->nqhd", grad_scores, key_part, preferred_element_type=jnp.float32)
        )
        key_add = jnp.einsum(
            "nhqk,nqhd->nkd", grad_scores, query_part, preferred_element_type=jnp.float32
        )
        value_add = jnp.einsum(
            "nhqk,nqhd->nkd", prob_low, grad_part, preferred_element_type=jnp.float32
        )
        pad_len = seq_len - key_len
        grad_keys = grad_keys + jnp.pad(key_add, ((0, 0), (0, pad_len), (0, 0)))
        grad_values = grad_values + jnp.pad(value_add, ((0, 0), (0, pad_len), (0, 0)))
    grad_query = jnp.concatenate(grad_queries, axis=1).reshape(all_rows, heads_here, head_dim)
    grad_qnorm = rotate_back(grad_query, cos_three, sine_three)
    grad_query_gain = jnp.sum(grad_qnorm * query_raw * query_scale, axis=(0, 1))
    grad_query_low = (
        norm_backward(grad_qnorm, query_raw, query_scale, query_gain)
        .astype(jnp.bfloat16)
        .reshape(all_rows, heads_here * head_dim)
    )
    grad_knorm = rotate_back(grad_keys.reshape(all_rows, head_dim), cos_table, sine_table)
    grad_key_gain = jnp.sum(grad_knorm * key_raw * key_scale, axis=0)
    grad_key_low = norm_backward(grad_knorm, key_raw, key_scale, key_gain).astype(jnp.bfloat16)
    grad_value_low = grad_values.reshape(all_rows, head_dim).astype(jnp.bfloat16)
    grad_wquery = jnp.einsum(
        "td,th->dh", gathered, grad_query_low, preferred_element_type=jnp.float32
    )
    key_block = jnp.einsum("td,th->dh", gathered, grad_key_low, preferred_element_type=jnp.float32)
    value_block = jnp.einsum(
        "td,th->dh", gathered, grad_value_low, preferred_element_type=jnp.float32
    )
    for bit in reversed(range(bit_count)):
        half_width = key_block.shape[1] // 2
        upper_side = group_index // 2**bit % 2 == 1
        key_keep = jnp.where(upper_side, key_block[:, half_width:], key_block[:, :half_width])
        key_send = jnp.where(upper_side, key_block[:, :half_width], key_block[:, half_width:])
        value_keep = jnp.where(upper_side, value_block[:, half_width:], value_block[:, :half_width])
        value_send = jnp.where(upper_side, value_block[:, :half_width], value_block[:, half_width:])
        key_got, value_got = (
            swapped(key_send.astype(jnp.bfloat16), "expert", bit).astype(key_send.dtype),
            swapped(value_send.astype(jnp.bfloat16), "expert", bit).astype(value_send.dtype),
        )
        key_block = key_keep + key_got
        value_block = value_keep + value_got
    grad_wq, grad_wk, grad_wv, grad_wo = (
        lax.psum_scatter(
            grad_wquery.astype(jnp.bfloat16), "dp", scatter_dimension=0, tiled=True
        ).astype(jnp.float32),
        lax.psum_scatter(
            key_block.astype(jnp.bfloat16), "dp", scatter_dimension=0, tiled=True
        ).astype(jnp.float32),
        lax.psum_scatter(
            value_block.astype(jnp.bfloat16), "dp", scatter_dimension=0, tiled=True
        ).astype(jnp.float32),
        lax.psum_scatter(
            grad_wout.astype(jnp.bfloat16), "dp", scatter_dimension=1, tiled=True
        ).astype(jnp.float32),
    )
    total_term = jnp.einsum("th,dh->td", grad_query_low, q_cols, preferred_element_type=jnp.float32)
    total_term = total_term + jnp.einsum(
        "th,dh->td", grad_key_low, k_head, preferred_element_type=jnp.float32
    )
    grad_normed = lax.psum_scatter(
        (
            total_term
            + jnp.einsum("th,dh->td", grad_value_low, v_head, preferred_element_type=jnp.float32)
        ).astype(jnp.bfloat16),
        "expert",
        scatter_dimension=0,
        tiled=True,
    ).astype(jnp.float32)
    grad_norm1 = jnp.sum(grad_normed * token_f * first_scale, axis=0)
    grad_tokens = grad_hidden + norm_backward(grad_normed, token_f, first_scale, norm1_gain)
    small_sums = lax.psum(
        (grad_norm1, grad_query_gain, grad_key_gain, grad_norm2, grad_router), ("dp", "expert")
    )
    return (
        output,
        grad_tokens,
        small_sums[0],
        grad_wq,
        grad_wk,
        grad_wv,
        grad_wo,
        small_sums[1],
        small_sums[2],
        small_sums[3],
        small_sums[4],
        grad_gate_w,
        grad_up_w,
        grad_down,
    )


def solution(mesh):
    placed = (
        P(("dp", "expert"), None),
        P(),
        P("dp", "expert"),
        P("dp", "expert"),
        P("dp", "expert"),
        P("expert", "dp"),
        P(),
        P(),
        P(),
        P(),
        P(("dp", "expert"), None, None),
        P(("dp", "expert"), None, None),
        P(("dp", "expert"), None, None),
        P(("dp", "expert"), None),
        P(("dp", "expert"), None),
    )
    return jax.shard_map(
        local,
        mesh=mesh,
        in_specs=placed,
        out_specs=(
            P(("dp", "expert"), None),
            P(("dp", "expert"), None),
            P(),
            P("dp", "expert"),
            P("dp", "expert"),
            P("dp", "expert"),
            P("expert", "dp"),
            P(),
            P(),
            P(),
            P(),
            P(("dp", "expert"), None, None),
            P(("dp", "expert"), None, None),
            P(("dp", "expert"), None, None),
        ),
        check_vma=False,
    )
```

profile of v0, /device:TPU:0, one launch (start us, length us, event | category | flops | bytes accessed | tf_op | source)
XLA Modules:
  0.0 1269.0 jit_solution(2618326366141485629)
XLA Ops:
  12.0 15.8 %all_gather.20 = bf16[2048,64]{0,1:T(8,128)(2,1)S(1)} all-gather(bf16[512,64]{0,1:T(8,128)(2,1)} %param.18), channel_id=1, replica_groups=mesh['dp'=4,'expert'=8] {'dp'}, dimensions={0}, use_global_device_ids=true | all-gather | bytes 327680 | tf_op jit(solution)/shard_map/all_gather | solution.py:98
  27.9 16.8 %all_gather.19 = bf16[2048,64]{0,1:T(8,128)(2,1)} all-gather(bf16[512,64]{0,1:T(8,128)(2,1)} %param.19), channel_id=1, replica_groups=mesh['dp'=4,'expert'=8] {'dp'}, dimensions={0}, use_global_device_ids=true | all-gather | bytes 327680 | tf_op jit(solution)/shard_map/all_gather | solution.py:99
  62.7 35.6 %all-gather.7.cloned.1.call-done = bf16[2048,512]{1,0:T(8,128)(2,1)} async-done(((bf16[512,512]{1,0:T(8,128)(2,1)}), bf16[2048,512]{1,0:T(8,128)(2,1)}) %all-gather.7.cloned.1.call-update) | async-done | bytes 2097168 | tf_op jit(solution)/shard_map/all_gather | solution.py:97
  134.8 9.8 all-gather.9.cloned.1.call-done
  153.1 9.0 reduce-window.6
  162.9 59.5 %reduce-scatter.7.cloned.1.call-done = f32[128,2048]{1,0:T(8,128)} async-done(((f32[1024,2048]{1,0:T(8,128)}), f32[128,2048]{1,0:T(8,128)}) %reduce-scatter.7.cloned.1.call-update) | async-done | bytes 1048592 | tf_op jit(solution)/shard_map/reduce_scatter | solution.py:176
  225.9 24.4 %scatter_custom_fusion = bf16[1152,2048]{1,0:T(8,128)(2,1)} fusion(s32[1024]{0:T(1024)S(1)} %bitcast.390, bf16[128,2048]{1,0:T(8,128)(2,1)} %multiply_convert_fusion.3, s32[1024]{0:T(1024)S(1)} %broadcast_clamp_fusion.1, bf16[]{:T(256)} %constant.105.clone.1), kind=kCustom, calls=%fused_computation.44 | custom fusion | bytes 4719104 | tf_op jit(solution)/shard_map/scatter | solution.py:198
  257.5 121.3 %all_to_all.20 = bf16[32,36,2048]{2,1,0:T(8,128)(2,1)} all-to-all(bf16[32,36,2048]{2,1,0:T(8,128)(2,1)} %reshape.525), channel_id=1, replica_groups=mesh['dp'=4,'expert'=8] {'dp','expert'}, dimensions={0} | all-to-all | bytes 9437184 | tf_op jit(solution)/shard_map/all_to_all | solution.py:60
  421.0 112.3 %all-to-all-done.1 = bf16[32,36,2048]{2,1,0:T(8,128)(2,1)} async-done(((bf16[32,36,2048]{2,1,0:T(8,128)(2,1)}), bf16[32,36,2048]{2,1,0:T(8,128)(2,1)}, u32[]{:S(2)}, u32[]{:S(2)}) %all-to-all-start.1) | async-done | bytes 4718624 | tf_op jit(solution)/shard_map/all_to_all | solution.py:60
  540.6 11.8 gather_fusion
  556.0 10.2 scatter_custom_fusion.1
  573.4 120.0 %all_to_all.21 = bf16[32,36,2048]{2,1,0:T(8,128)(2,1)} all-to-all(bf16[32,36,2048]{2,1,0:T(8,128)(2,1)} %reshape.530), channel_id=1, replica_groups=mesh['dp'=4,'expert'=8] {'dp','expert'}, dimensions={0} | all-to-all | bytes 9437184 | tf_op jit(solution)/shard_map/all_to_all | solution.py:60
  700.6 8.4 multiply_convert_fusion
  730.5 116.0 %all-to-all-done.3 = bf16[32,36,2048]{2,1,0:T(8,128)(2,1)} async-done(((bf16[32,36,2048]{2,1,0:T(8,128)(2,1)}), bf16[32,36,2048]{2,1,0:T(8,128)(2,1)}, u32[]{:S(2)}, u32[]{:S(2)}) %all-to-all-start.3) | async-done | bytes 4718624 | tf_op jit(solution)/shard_map/all_to_all | solution.py:60
  846.5 7.6 reshape.533
  854.1 11.8 gather_fusion.1
  874.1 35.1 %all-gather.11.cloned.1.call-done = bf16[1024,2048]{1,0:T(8,128)(2,1)} async-done(((bf16[128,2048]{1,0:T(8,128)(2,1)}), bf16[1024,2048]{1,0:T(8,128)(2,1)}) %all-gather.11.cloned.1.call-update) | async-done | bytes 4194320 | tf_op jit(solution)/shard_map/all_gather | solution.py:268
  991.4 8.9 convolution_bitcast_fusion
  1000.2 8.6 convolution_bitcast_fusion.1
  1018.3 11.6 reduce-scatter.11.cloned.1.call-done
  1032.0 43.4 %reduce-scatter.17.cloned.1.call-done = bf16[512,512]{1,0:T(8,128)(2,1)} async-done(((bf16[512,2048]{1,0:T(8,128)(2,1)}), bf16[512,512]{1,0:T(8,128)(2,1)}) %reduce-scatter.17.cloned.1.call-update) | async-done | bytes 524304 | tf_op jit(solution)/shard_map/reduce_scatter | solution.py:342
  1077.7 52.0 %reduce-scatter.9.cloned.1.call-done = bf16[128,2048]{1,0:T(8,128)(2,1)} async-done(((bf16[1024,2048]{1,0:T(8,128)(2,1)}), bf16[128,2048]{1,0:T(8,128)(2,1)}) %reduce-scatter.9.cloned.1.call-update) | async-done | bytes 524304 | tf_op jit(solution)/shard_map/reduce_scatter | solution.py:350
  1135.7 39.8 %all-reduce.2 = (f32[2048]{0:T(1024)}, f32[128]{0:T(128)}, f32[128]{0:T(128)}, f32[2048]{0:T(1024)}) all-reduce(f32[2048]{0:T(1024)S(1)} %get-tuple-element.18, f32[128]{0:T(128)S(1)} %bitcast_reduce_fusion, f32[128]{0:T(128)S(1)} %copy-done.71, f32[2048]{0:T(1024)S(1)} %copy-done.54), channel_id=1, replica_groups=mesh['dp'=4,'expert'=8] {'dp','expert'}, use_global_device_ids=true, to_apply=%region_27.28 | all-reduce | flops 4352 | bytes 34816 | tf_op jit(solution)/shard_map/psum | solution.py:361
  1175.5 85.2 %all-reduce.5.cloned.1.call-done = f32[2048,32]{0,1:T(8,128)} async-done(((f32[2048,32]{0,1:T(8,128)}), f32[2048,32]{0,1:T(8,128)}) %all-reduce.5.cloned.1.call-update) | async-done | bytes 262160 | tf_op jit(solution)/shard_map/psum | solution.py:361
  (338 shorter events, 278.8 us)
Async XLA Ops:
  7.2 392.8 %copy-start = (bf16[1,768,2048]{2,1,0:T(8,128)(2,1)S(1)}, bf16[1,768,2048]{2,1,0:T(8,128)(2,1)}, u32[]{:S(2)}) copy-start(bf16[1,768,2048]{2,1,0:T(8,128)(2,1)} %param.27) | copy-start | bytes 9437188
  7.2 43.6 %all-gather.5.cloned.1.call-start = ((), (), s32[]{:S(2)}) async-start(), calls=%async_computation.10 | async-start | bytes 4718592 | tf_op jit(solution)/shard_map/all_gather | solution.py:93
  11.2 87.1 %all-gather.7.cloned.1.call-start = ((), (), s32[]{:S(2)}) async-start(), calls=%async_computation.11 | async-start | bytes 2621440 | tf_op jit(solution)/shard_map/all_gather | solution.py:97
  12.0 132.6 %all-gather.9.cloned.1.call-start = ((), (), s32[]{:S(2)}) async-start(), calls=%async_computation.12 | async-start | bytes 2621440 | tf_op jit(solution)/shard_map/all_gather | solution.py:100
  27.9 18.9 %collective-permute-start.1 = (bf16[2048,64]{0,1:T(8,128)(2,1)S(1)}, bf16[2048,64]{0,1:T(8,128)(2,1)}, u32[]{:S(2)}, u32[]{:S(2)}) collective-permute-start(bf16[2048,64]{0,1:T(8,128)(2,1)S(1)} %all_gather.20), channel_id=1, source_target_pairs={{0,1},{1,0},{2,3},{3,2},{4,5},{5,4},{6,7},{7,6},{8,9},{9,8},{10,11... | collective-permute-start | bytes 786440 | tf_op jit(solution)/shard_map/ppermute | solution.py:20
  44.7 75.5 %collective-permute-start = (bf16[2048,64]{0,1:T(8,128)(2,1)}, bf16[2048,64]{0,1:T(8,128)(2,1)}, u32[]{:S(2)}, u32[]{:S(2)}) collective-permute-start(bf16[2048,64]{0,1:T(8,128)(2,1)} %all_gather.19), channel_id=1, source_target_pairs={{0,1},{1,0},{2,3},{3,2},{4,5},{5,4},{6,7},{7,6},{8,9},{9,8},{10,11... | collective-permute-start | bytes 786440 | tf_op jit(solution)/shard_map/ppermute | solution.py:20
  44.7 177.8 %reduce-scatter.7.cloned.1.call-start = ((), (), s32[]{:S(2)}) async-start(), calls=%async_computation.13 | async-start | bytes 9437184 | tf_op jit(solution)/shard_map/reduce_scatter | solution.py:176
  412.6 120.8 %all-to-all-start.1 = ((bf16[32,36,2048]{2,1,0:T(8,128)(2,1)}), bf16[32,36,2048]{2,1,0:T(8,128)(2,1)}, u32[]{:S(2)}, u32[]{:S(2)}) async-start(bf16[32,36,2048]{2,1,0:T(8,128)(2,1)} %reshape.527), calls=%async_computation.2 | async-start | bytes 10485760 | tf_op jit(solution)/shard_map/all_to_all | solution.py:60
  725.9 120.6 %all-to-all-start.3 = ((bf16[32,36,2048]{2,1,0:T(8,128)(2,1)}), bf16[32,36,2048]{2,1,0:T(8,128)(2,1)}, u32[]{:S(2)}, u32[]{:S(2)}) async-start(bf16[32,36,2048]{2,1,0:T(8,128)(2,1)} %reshape.532), calls=%async_computation.4 | async-start | bytes 10485760 | tf_op jit(solution)/shard_map/all_to_all | solution.py:60
  729.8 179.4 %all-gather.11.cloned.1.call-start = ((), (), s32[]{:S(2)}) async-start(), calls=%async_computation.14 | async-start | bytes 4718592 | tf_op jit(solution)/shard_map/all_gather | solution.py:268
  873.4 141.9 %reduce-scatter.15.cloned.1.call-start = ((), (), s32[]{:S(2)}) async-start(), calls=%async_computation.18 | async-start | bytes 327680 | tf_op jit(solution)/shard_map/reduce_scatter | solution.py:339
  926.3 17.3 %collective-permute-start.3 = (bf16[2048,64]{0,1:T(8,128)(2,1)}, bf16[2048,64]{0,1:T(8,128)(2,1)}, u32[]{:S(2)}, u32[]{:S(2)}) collective-permute-start(bf16[2048,64]{0,1:T(8,128)(2,1)} %select_convert_fusion), channel_id=1, source_target_pairs={{0,1},{1,0},{2,3},{3,2},{4,5},{5,4},{6,7},{7,6},{8,9},{9,8},{10,11... | collective-permute-start | bytes 786440 | tf_op jit(solution)/shard_map/ppermute | solution.py:20
  938.4 20.6 %collective-permute-start.2 = (bf16[2048,64]{0,1:T(8,128)(2,1)}, bf16[2048,64]{0,1:T(8,128)(2,1)}, u32[]{:S(2)}, u32[]{:S(2)}) collective-permute-start(bf16[2048,64]{0,1:T(8,128)(2,1)} %select_convert_fusion.1), channel_id=1, source_target_pairs={{0,1},{1,0},{2,3},{3,2},{4,5},{5,4},{6,7},{7,6},{8,9},{9,8},{10,11... | collective-permute-start | bytes 786440 | tf_op jit(solution)/shard_map/ppermute | solution.py:20
  945.3 71.5 %reduce-scatter.13.cloned.1.call-start = ((), (), s32[]{:S(2)}) async-start(), calls=%async_computation.17 | async-start | bytes 327680 | tf_op jit(solution)/shard_map/reduce_scatter | solution.py:336
  960.7 69.2 %reduce-scatter.11.cloned.1.call-start = ((), (), s32[]{:S(2)}) async-start(), calls=%async_computation.16 | async-start | bytes 2621440 | tf_op jit(solution)/shard_map/reduce_scatter | solution.py:333
  967.1 108.3 %reduce-scatter.17.cloned.1.call-start = ((), (), s32[]{:S(2)}) async-start(), calls=%async_computation.19 | async-start | bytes 2621440 | tf_op jit(solution)/shard_map/reduce_scatter | solution.py:342
  973.2 156.5 %reduce-scatter.9.cloned.1.call-start = ((), (), s32[]{:S(2)}) async-start(), calls=%async_computation.15 | async-start | bytes 4718592 | tf_op jit(solution)/shard_map/reduce_scatter | solution.py:350
  982.7 278.0 %all-reduce.5.cloned.1.call-start = ((), (), s32[]{:S(2)}) async-start(), calls=%async_computation.20 | async-start | bytes 524288 | tf_op jit(solution)/shard_map/psum | solution.py:361
  1008.9 120.8 %copy-start.47 = (f32[2048]{0:T(1024)S(1)}, f32[2048]{0:T(1024)}, u32[]{:S(2)}) copy-start(f32[2048]{0:T(1024)} %param.16) | copy-start | bytes 24580
  1008.9 120.7 %copy-start.68 = (f32[128]{0:T(128)S(1)}, f32[128]{0:T(128)}, u32[]{:S(2)}) copy-start(f32[128]{0:T(128)} %copy-done.67) | copy-start | bytes 1540
  1015.2 116.0 %copy-start.44 = (f32[2048]{0:T(1024)S(1)}, f32[2048]{0:T(1024)}, u32[]{:S(2)}) copy-start(f32[2048]{0:T(1024)} %param.23) | copy-start | bytes 24580
  1015.2 116.0 %copy-start.60 = (f32[128]{0:T(128)S(1)}, f32[128]{0:T(128)}, u32[]{:S(2)}) copy-start(f32[128]{0:T(128)} %copy-done.58) | copy-start | bytes 1540
  1015.2 116.0 %copy-start.70 = (f32[128]{0:T(128)S(1)}, f32[128]{0:T(128)}, u32[]{:S(2)}) copy-start(f32[128]{0:T(128)} %copy-done.69) | copy-start | bytes 1540
  1075.4 187.0 %copy-start.1 = (bf16[1,768,2048]{2,1,0:T(8,128)(2,1)S(1)}, bf16[1,768,2048]{2,1,0:T(8,128)(2,1)}, u32[]{:S(2)}) copy-start(bf16[1,768,2048]{2,1,0:T(8,128)(2,1)} %param.27) | copy-start | bytes 9437188
  (80 other events, 817.4 us)
Sparse Core Ops, SparseCore 0:
  11.3 39.4 all-gather.4
  52.4 45.9 all-gather.6
  99.9 44.6 all-gather.8
  152.3 70.0 reduce-scatter.6
  873.5 35.6 all-gather.10
  945.4 19.5 reduce-scatter.14
  967.3 17.9 reduce-scatter.12
  987.7 42.1 reduce-scatter.10
  1032.2 43.1 reduce-scatter.16
  1079.0 50.6 reduce-scatter.8
  1135.7 124.9 all-reduce.4
where the time goes:
time: 1280 us; the launch traced here: 1270 us
  waiting for transfers between devices  565 us (44%)
  blocking collectives  314 us (25%)
  matrix products  138 us (11%)
  local copies, waits for them, and re-layouts  136 us (11%)
  other arithmetic  90.7 us (7%)
  between operations  15.3 us (1%)
    all_to_all x2, blocking collectives, move_rows(): lax.all_to_all(buffer, ('dp', 'expert'), split_axis=0, concat_axis=0, til...  241 us
    all_to_all x2, waiting for transfers between devices, move_rows(): lax.all_to_all(buffer, ('dp', 'expert'), split_axis=0, concat_axis=0, til...  228 us
    psum x1, waiting for transfers between devices, local(): lax.psum((grad_norm1, grad_query_gain, grad_key_gain, grad_norm2, grad_ro...  85.2 us
    reduce_scatter x1, waiting for transfers between devices, local(): lax.psum_scatter(jnp.dot(attended, o_rows, preferred_element_type=jnp.flo...  59.5 us
    reduce_scatter x1, waiting for transfers between devices, local(): lax.psum_scatter((total_term + jnp.einsum('th,dh->td', grad_value_low, v_...  52 us
    reduce_scatter x1, waiting for transfers between devices, local(): lax.psum_scatter(grad_wout.astype(jnp.bfloat16), 'dp', scatter_dimension=...  43.4 us
    psum x1, blocking collectives, local(): lax.psum((grad_norm1, grad_query_gain, grad_key_gain, grad_norm2, grad_ro...  39.8 us
    all_gather x1, waiting for transfers between devices, local(): lax.all_gather(w_query, 'dp', axis=0, tiled=True)  35.6 us
  transfers between devices with their start and end apart: 17, of which 11 were waited for; matrix products, arithmetic and copies ran while one was open for 13% of the time, Pallas kernels for 0%

commit v1 on v0

v1 whole, which is shorter than its diff:
```python
import jax
import jax.numpy as jnp
import numpy as np
from jax import lax
from jax.experimental import pallas as pl
from jax.experimental.pallas import tpu as pltpu
from jax.sharding import PartitionSpec as P

SEQ_LEN = 1024


NORM_EPS = 1e-06
ROPE_THETA = 1000000.0
LOG2_E = 1.4426950408889634


def whole_up(value, unit):
    return -(-value // unit) * unit


def whole_up(value, unit):
    return -(-value // unit) * unit


VMEM_LIMIT = 61 * 1024 * 1024


def flipped(index, mask):
    moved = index
    bit = 1
    while bit <= mask:
        if mask & bit:
            moved = moved + bit * (1 - 2 * ((index // bit) % 2))
        bit *= 2
    return moved


def remote(src, dst, send_sem, recv_sem, axis, target):
    return pltpu.make_async_remote_copy(
        src_ref=src,
        dst_ref=dst,
        send_sem=send_sem,
        recv_sem=recv_sem,
        device_id={axis: target},
        device_id_type=pl.DeviceIdType.MESH,
    )


def greet(line=True, plane=True, far=False):
    barrier = pltpu.get_barrier_semaphore()
    count = 0
    if line:
        size, me = lax.axis_size("dp"), lax.axis_index("dp")
        for step in range(1, size) if far else (1, size - 1):
            pl.semaphore_signal(
                barrier,
                inc=1,
                device_id={"dp": (me + step) % size},
                device_id_type=pl.DeviceIdType.MESH,
            )
            count += 1
    if plane:
        size, me = lax.axis_size("expert"), lax.axis_index("expert")
        for mask in range(1, size):
            pl.semaphore_signal(
                barrier,
                inc=1,
                device_id={"expert": flipped(me, mask)},
                device_id_type=pl.DeviceIdType.MESH,
            )
            count += 1
    pl.semaphore_wait(barrier, count)


class LineGather:
    def __init__(self, own, slot, sems):
        self.size, self.me = lax.axis_size("dp"), lax.axis_index("dp")
        self.own, self.slot, self.sems = own, slot, sems

    def copy(self, way, k, s, src, block):
        target = self.me + 1 if way == 0 else self.me - 1
        dst = self.slot(k, block)
        return remote(src, dst, self.sems.at[way, k, s], self.sems.at[2 + way, k, s], "dp", target)

    def can_send(self, way, s):
        if way == 0:
            return (self.me < self.size - 1) & (self.me - s >= 0)
        return (self.me > 0) & (self.me + s < self.size)

    def start(self, k):
        for way in range(2):

            @pl.when(self.can_send(way, 0))
            def _():
                self.copy(way, k, 0, self.own(k), self.me).start()

    def step(self, k, s):
        for way in range(2):
            block = self.me - s if way == 0 else self.me + s
            present = block >= 0 if way == 0 else block < self.size

            @pl.when(present)
            def _():
                self.copy(way, k, s - 1, self.slot(k, block), block).wait_recv()

            if s < self.size - 1:

                @pl.when(self.can_send(way, s))
                def _():
                    self.copy(way, k, s, self.slot(k, block), block).start()

    def finish(self, k):
        for s in range(self.size - 1):
            for way in range(2):

                @pl.when(self.can_send(way, s))
                def _():
                    self.copy(way, k, s, self.own(k), self.me).wait_send()

    def run(self, count, window, done):
        for k in range(min(window, count)):
            self.start(k)
        for k in range(count):
            for s in range(1, self.size):
                self.step(k, s)
            if k + window < count:
                self.start(k + window)
            done(k)
        for k in range(count):
            self.finish(k)


class LineReduce:
    def __init__(self, part, inbox, sems):
        self.size, self.me = lax.axis_size("dp"), lax.axis_index("dp")
        self.part, self.inbox, self.sems = part, inbox, sems

    def copy(self, way, k, j):
        target = self.me + 1 if way == 0 else self.me - 1
        return remote(
            self.part(k, j),
            self.inbox(way, k, j),
            self.sems.at[way, k, j],
            self.sems.at[2 + way, k, j],
            "dp",
            target,
        )

    def begin(self, k):
        last = self.size - 1
        for turn in range(last):
            for way, j, end in ((0, last - turn, 0), (1, turn, last)):

                @pl.when(self.me == end)
                def _():
                    self.copy(way, k, j).start()

    def begin_block(self, k, j):
        for way, end in ((0, 0), (1, self.size - 1)):
            if j != end:

                @pl.when(self.me == end)
                def _():
                    self.copy(way, k, j).start()

    def sweep(self, k, way):
        last = self.size - 1
        for turn in range(last):
            j = last - turn if way == 0 else turn
            inner = (self.me > 0) if way == 0 else (self.me < last)
            passing = (j > self.me) if way == 0 else (j < self.me)

            @pl.when(inner & (passing | (self.me == j)))
            def _():
                self.copy(way, k, j).wait_recv()

            @pl.when(inner & passing)
            def _():
                total = self.part(k, j)[...].astype(jnp.float32) + self.inbox(way, k, j)[
                    ...
                ].astype(jnp.float32)
                self.part(k, j)[...] = total.astype(self.part(k, j).dtype)
                self.copy(way, k, j).start()

    def near(self, k):
        @pl.when(self.me < self.size // 2)
        def _():
            self.sweep(k, 0)

        @pl.when(self.me >= self.size // 2)
        def _():
            self.sweep(k, 1)

    def far(self, k):
        @pl.when(self.me < self.size // 2)
        def _():
            self.sweep(k, 1)

        @pl.when(self.me >= self.size // 2)
        def _():
            self.sweep(k, 0)

    def result(self, k, out):
        last = self.size - 1
        out[...] = self.part(k, self.me)[...].astype(jnp.float32)

        @pl.when(self.me > 0)
        def _():
            out[...] += self.inbox(0, k, self.me)[...].astype(jnp.float32)

        @pl.when(self.me < last)
        def _():
            out[...] += self.inbox(1, k, self.me)[...].astype(jnp.float32)

    def finish(self, k):
        last = self.size - 1
        for j in range(self.size):
            for way in range(2):
                sent = (j > self.me) if way == 0 else (j < self.me)

                @pl.when(sent)
                def _():
                    self.copy(way, k, j).wait_send()


def bit_orders(size):
    bits = [1 << i for i in range(size.bit_length() - 1)]
    bits.reverse()
    half = max(1, len(bits) // 2)
    if len(bits) == 3:
        return [bits, [bits[1], bits[0], bits[2]]]
    return [bits, bits[half:] + bits[:half]]


class PlaneGather:
    def __init__(self, own, slot, sems, orders):
        self.size, self.me = lax.axis_size("expert"), lax.axis_index("expert")
        self.own, self.slot, self.sems, self.orders = own, slot, sems, orders

    def place(self, h, mask):
        return max(at for at, bit in enumerate(self.orders[h]) if mask & bit)

    def copy(self, h, mask):
        last = self.orders[h][self.place(h, mask)]
        block = flipped(self.me, mask - last)
        src = self.own(h) if mask == last else self.slot(h, block)
        return remote(
            src,
            self.slot(h, block),
            self.sems.at[0, h, mask],
            self.sems.at[1, h, mask],
            "expert",
            flipped(self.me, last),
        )

    def wait(self, h, mask):
        here = self.slot(h, flipped(self.me, mask))
        remote(
            here, here, self.sems.at[0, h, mask], self.sems.at[1, h, mask], "expert", flipped(self.me, 1)
        ).wait_recv()

    def start(self, some=None):
        for at in range(len(self.orders[0])):
            for h, order in enumerate(self.orders):
                if some is None or h in some:
                    self.copy(h, order[at]).start()

    def moves(self):
        found = [(h, mask) for h in range(len(self.orders)) for mask in range(1, self.size)]
        found.sort(key=lambda move: (move[1].bit_count(), self.place(*move), move[0]))
        return found

    def move(self, h, mask):
        self.wait(h, mask)
        for bit in self.orders[h][self.place(h, mask) + 1 :]:
            self.copy(h, mask | bit).start()

    def relay(self):
        for h, mask in self.moves():
            self.move(h, mask)

    def finish(self):
        for h in range(len(self.orders)):
            for mask in range(1, self.size):
                self.copy(h, mask).wait_send()


class PlaneReduce:
    def __init__(self, acc, inbox, sems, orders):
        self.size, self.me = lax.axis_size("expert"), lax.axis_index("expert")
        self.acc, self.inbox, self.sems, self.orders = acc, inbox, sems, orders

    def masks(self, h, at):
        later = self.orders[h][at + 1 :]
        found = [0]
        for bit in later:
            found = found + [mask | bit for mask in found]
        return sorted(found, key=lambda mask: (mask == 0, self.first(h, mask) if mask else 0))

    def first(self, h, mask):
        return min(at for at, bit in enumerate(self.orders[h]) if mask & bit)

    def number(self, h, at, mask):
        before = sum(self.size >> (step + 1) for step in range(at))
        return before + sorted(self.masks(h, at)).index(mask)

    def copy(self, h, at, mask):
        bit = self.orders[h][at]
        n = self.number(h, at, mask)
        return remote(
            self.acc(h, flipped(self.me, mask | bit)),
            self.inbox(h, n),
            self.sems.at[0, h, n],
            self.sems.at[1, h, n],
            "expert",
            flipped(self.me, bit),
        )

    def start(self, h):
        for mask in self.masks(h, 0):
            self.copy(h, 0, mask).start()

    def advance(self, h, at):
        for mask in self.masks(h, at):
            self.copy(h, at, mask).wait_recv()
            if mask:
                here = self.acc(h, flipped(self.me, mask))
                arrived = self.inbox(h, self.number(h, at, mask))
                here[...] = (
                    here[...].astype(jnp.float32) + arrived[...].astype(jnp.float32)
                ).astype(here.dtype)
                if self.first(h, mask) == at + 1:
                    self.copy(h, at + 1, mask - self.orders[h][at + 1]).start()

    def result(self, h, out):
        total = self.acc(h, self.me)[...].astype(jnp.float32)
        for at in range(len(self.orders[h])):
            total = total + self.inbox(h, self.number(h, at, 0))[...].astype(jnp.float32)
        out[...] = total

    def finish(self, h):
        for at in range(len(self.orders[h])):
            for mask in self.masks(h, at):
                self.copy(h, at, mask).wait_send()


def part_of(ref, item, rows, width):
    chunk, low, wide = item
    if wide == width:
        return ref.at[chunk, rows]
    return ref.at[chunk, rows, pl.ds(low, wide)]


def halved(chunks, width, at):
    items = []
    for c in range(chunks):
        if c == at and width >= 256:
            items += [(c, 0, width // 2), (c, width // 2, width // 2)]
        else:
            items.append((c, 0, width))
    return items


def vmem(shape, dtype):
    return pltpu.VMEM(shape, dtype)


def dma(*shape):
    return pltpu.SemaphoreType.DMA(shape)


def call(kernel, outs, scratch, number, *operands):
    whole = pl.BlockSpec(memory_space=pltpu.VMEM)
    return pl.pallas_call(
        kernel,
        out_shape=outs,
        in_specs=[whole] * len(operands),
        out_specs=jax.tree.map(lambda _: whole, outs),
        scratch_shapes=scratch,
        compiler_params=pltpu.CompilerParams(
            collective_id=number, has_side_effects=True, vmem_limit_bytes=VMEM_LIMIT
        ),
    )(*operands)


class PlaneExchange:
    def __init__(self, src, dst, sems):
        self.size, self.me = lax.axis_size("expert"), lax.axis_index("expert")
        self.src, self.dst, self.sems = src, dst, sems

    def copy(self, k, peer):
        return remote(
            self.src(k, peer),
            self.dst(k, self.me),
            self.sems.at[0, k, peer],
            self.sems.at[1, k, self.me],
            "expert",
            peer,
        )

    def peers(self):
        order = sorted(range(1, self.size), key=lambda mask: (mask == 1, -mask.bit_count()))
        return [flipped(self.me, mask) for mask in order]

    def start(self, k):
        for peer in self.peers():
            self.copy(k, peer).start()

    def keep(self, k):
        self.dst(k, self.me)[...] = self.src(k, self.me)[...]

    def wait(self, k):
        for peer in self.peers():
            here = self.dst(k, peer)
            remote(
                here, here, self.sems.at[0, k, peer], self.sems.at[1, k, peer], "expert", peer
            ).wait_recv()

    def finish(self, k):
        for peer in self.peers():
            self.copy(k, peer).wait_send()


def combine(values, select, slots, number):
    data, group = lax.axis_size("dp"), lax.axis_size("expert")
    chunks, entries, width = values.shape
    rows = select.shape[1] // data
    window = 1

    def kernel(v_ref, select, out_ref, turned, back, part, inbox, ls, es):
        greet()
        exchange = PlaneExchange(
            lambda k, p: v_ref.at[k, pl.ds(pl.multiple_of(p * slots, slots), slots)],
            lambda k, p: back.at[k, pl.ds(pl.multiple_of(p * slots, slots), slots)],
            es,
        )
        line = LineReduce(
            lambda k, j: part.at[k, pl.ds(pl.multiple_of(j * rows, rows), rows)],
            lambda way, k, j: inbox.at[k, j + 1 - way],
            ls,
        )
        for k in range(window):
            exchange.start(k)
        turned[...] = select[...].T
        for k in range(chunks):
            exchange.keep(k)
        for k in range(chunks):
            exchange.wait(k)
            if k + window < chunks:
                exchange.start(k + window)
            total = jnp.dot(
                turned[...], back[k], preferred_element_type=jnp.float32
            )
            part[k] = total.astype(jnp.bfloat16)
            line.begin(k)
            line.near(k)
            if k:
                line.far(k - 1)
        line.far(chunks - 1)
        for k in range(chunks):
            line.result(k, out_ref.at[:, pl.ds(k * width, width)])
            line.finish(k)
            exchange.finish(k)

    return call(
        kernel,
        jax.ShapeDtypeStruct((rows, chunks * width), jnp.float32),
        [
            vmem(select.shape[::-1], jnp.bfloat16),
            vmem(values.shape, jnp.bfloat16),
            vmem((chunks, data * rows, width), jnp.bfloat16),
            vmem((chunks, data + 1, rows, width), jnp.bfloat16),
            dma(4, chunks, data),
            dma(2, chunks, group),
        ],
        number,
        values,
        select,
    )


def expert_layer(
    second, pair, probs, hidden, out_grad, gain, w_router, select, grads_here,
    w_gate, w_up, w_down, cut, with_mix,
):
    data, group = lax.axis_size("dp"), lax.axis_size("expert")
    chunks, rows, width = second.shape
    model = chunks * width
    experts = w_router.shape[0]
    extra = pair.shape[1]
    entries = select.shape[0]
    slots = entries // group
    hidden_units = w_gate.shape[1]
    block = 2 * slots
    pieces = model // cut
    early = max(1, chunks // 2)
    came = halved(chunks, width, 0)
    sent = halved(chunks, width, chunks - 1)

    def kernel(
        sec_ref, pair_ref, prob_ref, hid_ref, g_ref, gain_ref, r_ref, select, gh_any, wg_any, wu_any, wd_any,
        x_any, s_any, h_any, v_any, grad_hidden, branch_any, norm_sum, router_sum, turned_any, mix_out,
        x_all, pair_all, picked_pair, pair_here, rows_out, pair_out, back, pair_back,
        inbox, pair_box, summed, pair_sum, turned, low, wg, wu, wd,
        x_here, g_stage, s_stage, v_stage, h_stage,
        mix_back, loads, g_load, stores, keeps, ls, es, ls2, es2, es3,
    ):
        place, plane = lax.axis_index("dp"), lax.axis_index("expert")
        own = place * group + plane
        pairs = group // 2
        fetches = [
            pltpu.make_async_copy(src, dst, loads.at[at])
            for at, (src, dst) in enumerate(((wg_any, wg), (wu_any, wu), (wd_any, wd)))
        ]

        def block_at(step):
            mask, at, bit = pairs - 1 - step, 0, 1
            while bit < pairs:
                at = at + bit * ((plane // (2 * bit) + mask // bit) % 2)
                bit *= 2
            return at

        def block_rows(step):
            at = block_at(step)
            return pl.ds(pl.multiple_of(at * block, block), block)

        def load_grads(step):
            slot = step % 2
            return pltpu.make_async_copy(
                gh_any.at[:, block_rows(step)], g_stage.at[slot], g_load.at[slot]
            )

        def store_block(step):
            slot, here = step % 2, block_rows(step)
            return [
                pltpu.make_async_copy(s_stage.at[slot], s_any.at[:, here], stores.at[slot, 0]),
                pltpu.make_async_copy(v_stage.at[slot], v_any.at[:, here], stores.at[slot, 1]),
                pltpu.make_async_copy(h_stage.at[slot], h_any.at[:, here], stores.at[slot, 2]),
            ]

        load_grads(0).start()
        for fetch in fetches:
            fetch.start()
        mine = pl.ds(pl.multiple_of(place * rows, rows), rows)
        for c in range(chunks):
            x_all[c, mine] = sec_ref[c]
        pair_all[mine] = pair_ref[...]
        greet()

        def slot_rows(p):
            return pl.ds(pl.multiple_of(p * slots, slots), slots)

        def token_rows(j):
            return pl.ds(pl.multiple_of(j * rows, rows), rows)

        def pick(items, full, wide):
            return lambda k, p: (
                part_of(full, items[k], slot_rows(p), width)
                if k < len(items)
                else wide.at[slot_rows(p)]
            )

        exchange = PlaneExchange(
            pick(came, rows_out, picked_pair), pick(came, x_here, pair_here), es
        )

        def done(k):
            if k == 0:
                picked_pair[...] = jnp.dot(
                    select[...], pair_all[...], preferred_element_type=jnp.float32
                ).astype(jnp.bfloat16)
                exchange.start(len(came))
                exchange.keep(len(came))
            else:
                c, at, wide = came[k - 1]
                rows_out[c, :, at : at + wide] = jnp.dot(
                    select[...], x_all[c, :, at : at + wide], preferred_element_type=jnp.float32
                ).astype(jnp.bfloat16)
                exchange.start(k - 1)
                exchange.keep(k - 1)

        line = LineGather(
            lambda k: (
                pair_ref if k == 0 else part_of(sec_ref, came[k - 1], pl.ds(0, rows), width)
            ),
            lambda k, j: (
                pair_all.at[token_rows(j)]
                if k == 0
                else part_of(x_all, came[k - 1], token_rows(j), width)
            ),
            ls,
        )
        line.run(len(came) + 1, 3, done)
        turned[...] = select[...].T
        keep_turned = pltpu.make_async_copy(turned, turned_any, keeps.at[2])
        keep_turned.start()
        for fetch in fetches:
            fetch.wait()
        for k in range(len(came) + 1):
            exchange.wait(k)
        for k in range(len(came) + 1):
            exchange.finish(k)
        keep_rows = pltpu.make_async_copy(x_here, x_any, keeps.at[0])
        keep_rows.start()

        give_back = PlaneExchange(
            pick(sent, rows_out, pair_out), pick(sent, back, pair_back), es2
        )
        lane = lax.broadcasted_iota(jnp.int32, (block, extra), 1)

        def run_block(step, carry):
            at = block_at(step)
            here = block_rows(step)
            slot = step % 2
            load_grads(step).wait()

            @pl.when(step + 1 < pairs)
            def _():
                load_grads(step + 1).start()

            @pl.when(step >= 2)
            def _():
                for store in store_block(step - 2):
                    store.wait()

            chosen = (lane == own) | (lane == own + experts)
            prob = jnp.sum(
                jnp.where(chosen, pair_here[here].astype(jnp.float32), 0.0), axis=-1, keepdims=True
            )
            gate_h = jnp.zeros((block, hidden_units), jnp.float32)
            up_h = jnp.zeros((block, hidden_units), jnp.float32)
            for c in range(chunks):
                x = x_here[c, here]
                part = pl.ds(c * width, width)
                gate_h += jnp.dot(x, wg[part], preferred_element_type=jnp.float32)
                up_h += jnp.dot(x, wu[part], preferred_element_type=jnp.float32)
            sigmoid = jax.nn.sigmoid(gate_h)
            silu = gate_h * sigmoid
            active = (silu * up_h).astype(jnp.bfloat16)
            h_stage[slot, 0] = active
            grad_active = jnp.zeros((block, hidden_units), jnp.float32)
            slot_gate = jnp.zeros((block, 1), jnp.float32)
            for c in range(chunks):
                part = pl.ds(c * width, width)
                out = jnp.dot(active, wd[:, part], preferred_element_type=jnp.float32)
                out = out.astype(jnp.bfloat16).astype(jnp.float32)
                grad = g_stage[slot, c].astype(jnp.float32)
                slot_gate += jnp.sum(out * grad, axis=-1, keepdims=True)
                v_stage[slot, c] = (prob * out).astype(jnp.bfloat16)
                grad_slot = (prob * grad).astype(jnp.bfloat16)
                s_stage[slot, c] = grad_slot
                grad_active += nt_dot(grad_slot, wd[:, part])
            grad_gate_h = grad_active * up_h * sigmoid * (1.0 + gate_h * (1.0 - sigmoid))
            grad_gate_h = grad_gate_h.astype(jnp.bfloat16)
            grad_up_h = (grad_active * silu).astype(jnp.bfloat16)
            h_stage[slot, 1] = grad_gate_h
            h_stage[slot, 2] = grad_up_h
            for store in store_block(step):
                store.start()
            top = slot_gate.astype(jnp.bfloat16).astype(jnp.float32)
            pair_out[here] = (
                jnp.where(lane == own, top, 0.0)
                + jnp.where(lane == own + experts, slot_gate - top, 0.0)
            ).astype(jnp.bfloat16)
            for c in range(chunks):
                part = pl.ds(c * width, width)
                rows_out[c, here] = (
                    nt_dot(grad_gate_h, wg[part]) + nt_dot(grad_up_h, wu[part])
                ).astype(jnp.bfloat16)
            for member in range(2):
                peer = 2 * at + member

                @pl.when(peer != plane)
                def _():
                    for k in [len(sent)] + list(range(early)):
                        give_back.copy(k, peer).start()

            return carry

        lax.fori_loop(0, pairs, run_block, 0)
        keep_rows.wait()
        for step in range(max(0, pairs - 2), pairs):
            for store in store_block(step):
                store.wait()
        mix = PlaneExchange(
            lambda k, p: v_any.at[0, slot_rows(p)], lambda k, p: mix_back.at[slot_rows(p)], es3
        )
        own_mix = pltpu.make_async_copy(
            v_any.at[0, slot_rows(plane)], mix_back.at[slot_rows(plane)], keeps.at[3]
        ) if with_mix else None
        give_back.start(early)
        for k in range(len(sent) + 1):
            give_back.keep(k)
        sums = LineReduce(
            lambda k, j: (
                part_of(x_all, sent[k], token_rows(j), width)
                if k < len(sent)
                else pair_all.at[token_rows(j)]
            ),
            lambda way, k, j: (
                inbox.at[
                    sent[k][0], j + 1 - way, :, pl.ds(sent[k][1], sent[k][2])
                ]
                if k < len(sent)
                else pair_box.at[j + 1 - way]
            ),
            ls2,
        )
        order = [len(sent)] + list(range(len(sent)))
        for at, k in enumerate(order):
            give_back.wait(k)
            if k < len(sent):
                c, low_col, wide = sent[k]
                x_all[c, :, low_col : low_col + wide] = jnp.dot(
                    turned[...],
                    back[c, :, low_col : low_col + wide],
                    preferred_element_type=jnp.float32,
                ).astype(jnp.bfloat16)
            else:
                pair_all[...] = jnp.dot(
                    turned[...], pair_back[...], preferred_element_type=jnp.float32
                ).astype(jnp.bfloat16)
            sums.begin(k)
            if k < len(sent) and early + 1 + k < len(sent):
                give_back.start(early + 1 + k)
            if at >= 1:
                sums.near(order[at - 1])
            if at >= 2:
                sums.far(order[at - 2])
        if with_mix:
            mix.start(0)
            own_mix.start()
        sums.near(order[-1])
        for k in order[-2:]:
            sums.far(k)
        for k, (c, low_col, wide) in enumerate(sent):
            sums.result(k, summed.at[:, pl.ds(c * width + low_col, wide)])
        sums.result(len(sent), pair_sum)

        gate = prob_ref[...]
        grad_gate = pair_sum[:, 0:experts] + pair_sum[:, experts : 2 * experts]
        inner = jnp.sum(gate * grad_gate, axis=-1, keepdims=True)
        grad_logits = (gate * (grad_gate - inner)).astype(jnp.bfloat16)
        for c in range(chunks):
            part = pl.ds(c * width, width)
            router_sum[:, part] = lax.dot_general(
                grad_logits,
                sec_ref[c],
                (((0,), (0,)), ((), ())),
                preferred_element_type=jnp.float32,
            )
        grad_second = summed[...] + jnp.dot(
            grad_logits, r_ref[...], preferred_element_type=jnp.float32
        )
        state = hid_ref[...]
        scale = row_scale(state)
        norm_sum[...] = jnp.sum(grad_second * state * scale, axis=0, keepdims=True)
        scaled = grad_second * gain_ref[...]
        inner = jnp.mean(scaled * state, axis=-1, keepdims=True)
        total = scale * scaled - state * (scale * scale * scale * inner)
        total = total + g_ref[...].astype(jnp.float32)
        grad_hidden[...] = total
        total = total.astype(jnp.bfloat16)
        for piece in range(pieces):
            low[piece] = total[:, piece * cut : (piece + 1) * cut]
        keep_low = pltpu.make_async_copy(low, branch_any, keeps.at[1])
        keep_low.start()
        if with_mix:
            own_mix.wait()
            mix.wait(0)
            mix_out[...] = jnp.dot(
                turned[...], mix_back[...], preferred_element_type=jnp.float32
            ).astype(jnp.bfloat16)
            mix.finish(0)
        keep_turned.wait()
        keep_low.wait()
        for k in range(len(sent) + 1):
            sums.finish(k)
            give_back.finish(k)

    bf, fl = jnp.bfloat16, jnp.float32
    whole = pl.BlockSpec(memory_space=pltpu.VMEM)
    anywhere = pl.BlockSpec(memory_space=pl.ANY)
    outs = [
        jax.ShapeDtypeStruct((chunks, entries, width), bf),
        jax.ShapeDtypeStruct((chunks, entries, width), bf),
        jax.ShapeDtypeStruct((3, entries, hidden_units), bf),
        jax.ShapeDtypeStruct((chunks, entries, width), bf),
        jax.ShapeDtypeStruct((rows, model), fl),
        jax.ShapeDtypeStruct((pieces, rows, cut), bf),
        jax.ShapeDtypeStruct((1, model), fl),
        jax.ShapeDtypeStruct((experts, model), fl),
        jax.ShapeDtypeStruct(select.shape[::-1], bf),
        jax.ShapeDtypeStruct((data * rows if with_mix else 16, width), bf),
    ]
    results = list(pl.pallas_call(
        kernel,
        out_shape=outs,
        in_specs=[whole] * 8 + [anywhere] * 4,
        out_specs=[anywhere] * 4 + [whole, anywhere, whole, whole, anywhere, whole],
        scratch_shapes=[
            vmem((chunks, data * rows, width), bf),
            vmem((data * rows, extra), bf),
            vmem((entries, extra), bf),
            vmem((entries, extra), bf),
            vmem((chunks, entries, width), bf),
            vmem((entries, extra), bf),
            vmem((chunks, entries, width), bf),
            vmem((entries, extra), bf),
            vmem((chunks, data + 1, rows, width), bf),
            vmem((data + 1, rows, extra), bf),
            vmem((rows, model), fl),
            vmem((rows, extra), fl),
            vmem(select.shape[::-1], bf),
            vmem((pieces, rows, cut), bf),
            vmem((model, hidden_units), bf),
            vmem((model, hidden_units), bf),
            vmem((hidden_units, model), bf),
            vmem((chunks, entries, width), bf),
            vmem((2, chunks, block, width), bf),
            vmem((2, chunks, block, width), bf),
            vmem((2, chunks, block, width), bf),
            vmem((2, 3, block, hidden_units), bf),
            vmem((entries if with_mix else 16, width), bf),
            dma(3),
            dma(2),
            dma(2, 3),
            dma(4),
            dma(4, len(came) + 1, data - 1),
            dma(2, len(came) + 1, group),
            dma(4, len(sent) + 1, data),
            dma(2, len(sent) + 1, group),
            dma(2, 1, group),
        ],
        compiler_params=pltpu.CompilerParams(
            collective_id=3, has_side_effects=True, vmem_limit_bytes=VMEM_LIMIT
        ),
    )(
        second, pair, probs, hidden, out_grad, gain, w_router, select, grads_here,
        w_gate, w_up, w_down,
    ))
    return results


def expert_weight_grads(arrived, grad_arrived, low_rows, others, kv):
    chunks, entries, width = arrived.shape
    hidden_units = low_rows.shape[2]
    part = kv.shape[0] // 2
    passed = len(others) + 2

    def kernel(x_ref, s_ref, low_ref, *refs):
        sources = refs[:passed]
        gate_out, up_out, down_out = refs[passed : passed + 3]
        targets = refs[passed + 3 : 2 * passed + 3]
        turned = refs[2 * passed + 3]

        @pl.when(pl.program_id(0) == 0)
        def _():
            turned[...] = low_ref[0].T

        for source, target in zip(sources, targets):
            target[...] = source[...]
        x = x_ref[0].T
        gate_out[0] = jnp.dot(x, low_ref[1], preferred_element_type=jnp.float32)
        up_out[0] = jnp.dot(x, low_ref[2], preferred_element_type=jnp.float32)
        down_out[0] = jnp.dot(turned[...], s_ref[0], preferred_element_type=jnp.float32)

    rows = pl.BlockSpec((1, entries, width), lambda c: (c, 0, 0))
    tall = pl.BlockSpec((1, width, hidden_units), lambda c: (0, c, 0))

    def slab(lines, item, first=0):
        return pl.BlockSpec((lines // chunks, item.shape[1]), lambda c: (c + first, 0))

    slabs = [slab(item.shape[0], item) for item in others]
    half = slab(part, kv)
    return pl.pallas_call(
        kernel,
        grid=(chunks,),
        out_shape=[
            jax.ShapeDtypeStruct((1, chunks * width, hidden_units), jnp.float32),
            jax.ShapeDtypeStruct((1, chunks * width, hidden_units), jnp.float32),
            jax.ShapeDtypeStruct((1, hidden_units, chunks * width), jnp.float32),
        ]
        + [jax.ShapeDtypeStruct(item.shape, item.dtype) for item in others]
        + [jax.ShapeDtypeStruct((part, kv.shape[1]), kv.dtype)] * 2,
        in_specs=[rows, rows, pl.BlockSpec((3, entries, hidden_units), lambda c: (0, 0, 0))]
        + slabs
        + [half, slab(part, kv, chunks)],
        out_specs=[tall, tall, pl.BlockSpec((1, hidden_units, width), lambda c: (0, 0, c))]
        + slabs
        + [half, half],
        scratch_shapes=[vmem((hidden_units, entries), jnp.bfloat16)],
        compiler_params=pltpu.CompilerParams(vmem_limit_bytes=VMEM_LIMIT),
    )(arrived, grad_arrived, low_rows, *others, kv, kv)


def attention_backward(
    grad_branch, out_blocks, x, w_q, w_kv, q_raw, q_low, k_raw, k_low, v_low, lse, att,
    cos, sin, gain_q, gain_k, mixed, turned, tokens, gain, grad_hidden, hidden, norm2_sum, router_sum, first_mix,
    seq_len, with_mix,
):
    data, group = lax.axis_size("dp"), lax.axis_size("expert")
    pieces, rows, cut = grad_branch.shape
    chunks, total, width = x.shape
    model = chunks * width
    depth = model // data
    wide = w_q.shape[1]
    sharing, _, both, _ = w_kv.shape
    part = both // 2
    head = sharing * part
    heads = wide // head
    block = min(256, seq_len)
    scale = head ** (-0.5)
    entries = turned.shape[1]
    slots = entries // group
    orders = [order[::-1] for order in bit_orders(group)]
    orders = [orders[at % 2] for at in range(chunks)]
    steps = len(orders[0])

    def kernel(
        gb_ref, wo_any, x_any, wq_any, wkv_any, qr_any, ql_any, kr_any, kl_any, vl_any, lse_any, att_ref,
        cos_ref, sin_ref, gq_ref, gk_ref, mix_any, turned_any, tok_ref, gain_ref, gh_any, hid_ref, n2_ref, rt_any, fm_ref,
        tok_out, wo_out, wq_out, wkv_out, gq_out, gk_out, n1_out, n2_out, rt_out, layer_out,
        wo_ref, x_ref, wq_ref, wkv_ref, ql_ref, kr_ref, kl_ref, vl_ref, lse_ref, turned,
        big, row_terms, log_rows, dq_low, dk, dv, dkv_low, kv_box, raw_buf,
        wo_part, wo_box, w_part, w_box, kv_part, kv_inbox, dx_box, back,
        mix_part, mix_box, summed, dx_sum, vec, vec_plane, vec_half, vec_line, rt_acc, rt_box, rt_half, rt_line, gq_sum, gk_sum,
        loads, raw_load, keep_s, wo_s, w_s, kv_s, sib_s, dx_s, ex_s, mix_s, vp_s, vl_s, rp_s, rl_s, rg_s, gb_s,
    ):
        place, plane = lax.axis_index("dp"), lax.axis_index("expert")
        member = plane % sharing

        def branch(j):
            first = j * cut
            return big.at[first // width, :, pl.ds(first % width, cut)]

        fetches = [
            pltpu.make_async_copy(src, dst, loads.at[at])
            for at, (src, dst) in enumerate(
                (
                    (rt_any, rt_acc),
                    (wo_any, wo_ref),
                    (ql_any, ql_ref),
                    (kl_any, kl_ref),
                    (vl_any, vl_ref),
                    (lse_any, lse_ref),
                    (x_any, x_ref),
                    (kr_any, kr_ref),
                    (wq_any, wq_ref),
                    (wkv_any, wkv_ref),
                    (gh_any, tok_out),
                )
            )
        ]
        for fetch in fetches:
            fetch.start()
        if with_mix:
            turned_load = pltpu.make_async_copy(turned_any, turned, loads.at[len(fetches)])
            turned_load.start()

        def load_raw(h):
            mine = pl.ds(pl.multiple_of(h * head, head), head)
            return pltpu.make_async_copy(qr_any.at[:, mine], raw_buf.at[h % 2], raw_load.at[h % 2])

        load_raw(0).start()

        def slot_rows(p):
            return pl.ds(pl.multiple_of(p * slots, slots), slots)

        def token_rows(j):
            return pl.ds(pl.multiple_of(j * rows, rows), rows)

        exchange = PlaneExchange(
            lambda k, p: mix_any.at[k, slot_rows(p)], lambda k, p: back.at[k, slot_rows(p)], ex_s
        )
        wo_sum = LineReduce(
            lambda k, j: wo_part.at[j, pl.ds(k * (wide // 2), wide // 2)],
            lambda way, k, j: wo_box.at[j + 1 - way, pl.ds(k * (wide // 2), wide // 2)],
            wo_s,
        )
        w_sum = LineReduce(
            lambda k, j: w_part.at[k, j], lambda way, k, j: w_box.at[k, j + 1 - way], w_s
        )
        kv_sum = LineReduce(
            lambda k, j: kv_part.at[j], lambda way, k, j: kv_inbox.at[j + 1 - way], kv_s
        )
        reduce = PlaneReduce(
            lambda h, j: big.at[h, token_rows(j)], lambda h, n: dx_box.at[h, n], dx_s, orders
        )

        mix_sum = LineReduce(
            lambda k, j: mix_part.at[k, token_rows(j)],
            lambda way, k, j: mix_box.at[k, j + 1 - way],
            mix_s,
        )
        share = model // group

        def share_cols(j):
            return pl.ds(pl.multiple_of(j * share, share), share)

        router = PlaneReduce(
            lambda h, j: rt_acc.at[:, share_cols(j)], lambda h, n: rt_box.at[n], rp_s, orders[:1]
        )
        router_back = PlaneGather(
            lambda h: rt_half.at[1],
            lambda h, j: rt_out.at[:, share_cols(j)],
            rg_s,
            bit_orders(group)[:1],
        )

        def router_line(step):
            return remote(
                rt_half.at[0], rt_line.at[step], rl_s.at[0, step], rl_s.at[1, step],
                "dp", (place + step) % data,
            )

        def router_stage(at):
            if at < steps:
                router.advance(0, at)
            elif at == steps:
                router.result(0, rt_half.at[0])
                for step in range(1, data):
                    router_line(step).start()
            elif at == steps + 1:
                total = rt_half[0]
                for step in range(1, data):
                    router_line(step).wait_recv()
                    total = total + rt_line[step]
                rt_half[1] = total
                rt_out[:, share_cols(plane)] = total
                router_back.start()
            else:
                router_back.relay()

        def vec_across(mask):
            return remote(
                vec, vec_plane.at[mask], vp_s.at[0, mask], vp_s.at[1, mask],
                "expert", flipped(plane, mask),
            )

        def vec_along(step):
            return remote(
                vec_half, vec_line.at[step], vl_s.at[0, step], vl_s.at[1, step],
                "dp", (place + step) % data,
            )

        def x_block(j):
            first = j * depth
            inner = first % width
            return x_ref[first // width, :, inner : inner + depth]

        own_rows = token_rows(plane)
        for h in range(pieces):
            branch(h)[own_rows] = gb_ref[h]
        if with_mix:
            mix_part[0] = fm_ref[...]
        greet(far=True)
        if with_mix:
            mix_sum.begin(0)
        gather = PlaneGather(
            lambda h: gb_ref.at[h],
            lambda h, j: big.at[
                (h * cut) // width, token_rows(j), pl.ds((h * cut) % width, cut)
            ],
            gb_s,
            [bit_orders(group)[at % 2] for at in range(pieces)],
        )
        pairs = [range(h, min(h + 2, pieces)) for h in range(0, pieces, 2)]
        gather.start(pairs[0])
        fetches[0].wait()
        att_turned = att_ref[...].T

        def wo_piece(j):
            wo_part[j] = jnp.dot(
                att_turned, branch(j)[...], preferred_element_type=jnp.float32
            ).astype(jnp.bfloat16)
            for k in range(2):
                wo_sum.begin_block(k, j)

        for at, pair in enumerate(pairs):
            moves = [move for move in gather.moves() if move[0] in pair]
            first = [move for move in moves if move[1].bit_count() == 1]
            for move in first:
                gather.move(*move)
            if at + 1 < len(pairs):
                gather.start(pairs[at + 1])
            for move in moves[len(first) :]:
                gather.move(*move)
            for h in pair:
                wo_piece(h)
        router.start(0)
        if with_mix:
            if chunks > 1:
                exchange.start(1)
            mix_sum.near(0)
        fetches[1].wait()

        lane = lax.broadcasted_iota(jnp.int32, (block, head), 1)

        def attended_grad(at, carry):
            here = pl.ds(pl.multiple_of(at * block, block), block)
            value = jnp.zeros((block, wide), jnp.float32)
            for j in range(pieces):
                value += nt_dot(branch(j)[here], wo_ref[j])
            low = value.astype(jnp.bfloat16)
            dq_low[here] = low
            both_rows = low.astype(jnp.float32) * att_ref[here].astype(jnp.float32)
            terms = jnp.zeros((block, head), jnp.float32)
            for h in range(heads):
                term = jnp.sum(both_rows[:, h * head : (h + 1) * head], axis=-1, keepdims=True)
                terms = jnp.where(lane == h, term, terms)
            dk[here] = terms
            return carry

        lax.fori_loop(0, total // block, attended_grad, 0)
        for at in range(2, 7):
            fetches[at].wait()
        row_terms[...] = dk[...].T
        log_rows[...] = lse_ref[...].T * LOG2_E
        dk[...] = jnp.zeros_like(dk)
        dv[...] = jnp.zeros_like(dv)
        above = lax.broadcasted_iota(
            jnp.int32, (block, block), 0
        ) <= lax.broadcasted_iota(jnp.int32, (block, block), 1)

        def turned_dot(left, right):
            return lax.dot_general(
                left, right, (((0,), (0,)), ((), ())), preferred_element_type=jnp.float32
            )

        def unrotate(value, table):
            return value * cos_ref[table] - half_turn(value) * sin_ref[table]

        def norm_back(turned_grad, raw, gain):
            factor = row_scale(raw)
            gain_term = jnp.sum(turned_grad * raw * factor, axis=0, keepdims=True)
            scaled = turned_grad * gain
            inner = jnp.mean(scaled * raw, axis=-1, keepdims=True)
            return factor * scaled - raw * (factor * factor * factor * inner), gain_term

        gq_sum[...] = jnp.zeros_like(gq_sum)
        gk_sum[...] = jnp.zeros_like(gk_sum)

        def own_mix(k):
            return pltpu.make_async_copy(
                mix_any.at[k, slot_rows(plane)], back.at[k, slot_rows(plane)], keep_s.at[k]
            )

        def gather_mix(k):
            own_mix(k).wait()
            exchange.wait(k)
            mix_part[k] = jnp.dot(
                turned[...], back[k], preferred_element_type=jnp.float32
            ).astype(jnp.bfloat16)
            mix_sum.begin(k)

        if with_mix:
            for k in range(1, chunks):
                own_mix(k).start()
            turned_load.wait()
            mix_sum.far(0)

        def head_back(h, carry):
            mine = pl.ds(pl.multiple_of(h * head, head), head)
            load_raw(h).wait()

            @pl.when(h + 1 < heads)
            def _():
                load_raw(h + 1).start()

            for seq in range(total // seq_len):
                base = seq * seq_len
                for at in range(seq_len // block):
                    here = pl.ds(base + at * block, block)
                    query = ql_ref[here, mine]
                    grad = dq_low[here, mine]
                    log_sum = log_rows[pl.ds(h, 1), here]
                    row_term = row_terms[pl.ds(h, 1), here]
                    grad_query = jnp.zeros((block, head), jnp.float32)
                    for other in range(at + 1):
                        behind = pl.ds(base + other * block, block)
                        key = kl_ref[behind]
                        probs = jnp.exp2(nt_dot(key, query) * (scale * LOG2_E) - log_sum)
                        if other == at:
                            probs = jnp.where(above, probs, 0.0)
                        grad_probs = nt_dot(vl_ref[behind], grad)
                        grad_scores = (probs * (grad_probs - row_term)).astype(jnp.bfloat16)
                        dv[behind] += jnp.dot(
                            probs.astype(jnp.bfloat16), grad, preferred_element_type=jnp.float32
                        )
                        dk[behind] += jnp.dot(
                            grad_scores, query, preferred_element_type=jnp.float32
                        )
                        grad_query += turned_dot(grad_scores, key)
                    grad_query = grad_query * scale
                    table = pl.ds(at * block, block)
                    raw_grad, gain_term = norm_back(
                        unrotate(grad_query, table), raw_buf[h % 2, here], gq_ref[...]
                    )
                    gq_sum[...] += gain_term
                    dq_low[here, mine] = raw_grad.astype(jnp.bfloat16)
            low_turned = dq_low[:, mine].T
            for j in range(data):
                w_part[h, j] = jnp.dot(
                    low_turned, x_block(j), preferred_element_type=jnp.float32
                ).astype(jnp.bfloat16)
            w_sum.begin(h)

            if with_mix:

                @pl.when(h + 2 < chunks)
                def _():
                    exchange.start(h + 2)

            if with_mix and heads > 2:

                @pl.when((h >= 2) & (h - 1 < chunks))
                def _():
                    gather_mix(h - 1)

            @pl.when(h == heads - 2)
            def _():
                wo_sum.near(0)

            @pl.when(h == heads - 1)
            def _():
                wo_sum.near(1)
                wo_sum.far(0)

            return carry

        lax.fori_loop(0, heads, head_back, 0)
        if with_mix:
            for k in range(heads + 2, chunks):
                exchange.start(k)
        for at in range(7, len(fetches)):
            fetches[at].wait()
        for at in range(total // block):
            here = pl.ds(at * block, block)
            table = pl.ds((at * block) % seq_len, block)
            raw_grad, gain_term = norm_back(
                unrotate(dk[here] * scale, table), kr_ref[here], gk_ref[...]
            )
            gk_sum[...] += gain_term
            value_grad = dv[here]
            for m in range(sharing):
                cols = slice(m * part, (m + 1) * part)
                dkv_low[m, here] = jnp.concatenate(
                    [raw_grad[:, cols], value_grad[:, cols]], axis=1
                ).astype(jnp.bfloat16)

        def swap(mask):
            other = flipped(plane, mask)
            return remote(
                dkv_low.at[other % sharing],
                kv_box.at[member],
                sib_s.at[0, mask],
                sib_s.at[1, mask],
                "expert",
                other,
            )

        for mask in range(1, sharing):
            swap(mask).start()
        gather.finish()
        for j in range(data):
            first = j * depth
            c, inner = first // width, first % width

            def input_grad(at, carry):
                here = pl.ds(pl.multiple_of(at * block, block), block)
                value = nt_dot(dq_low[here], wq_ref[pl.ds(first, depth)])
                for m in range(sharing):
                    value += jnp.dot(
                        dkv_low[m, here], wkv_ref[m, j], preferred_element_type=jnp.float32
                    )
                big[c, here, inner : inner + depth] = value.astype(jnp.bfloat16)
                return carry

            lax.fori_loop(0, total // block, input_grad, 0)
            if inner + depth == width:
                reduce.start(c)
        kv_box[member] = dkv_low[member]
        for mask in range(1, sharing):
            other = kv_box.at[flipped(plane, mask) % sharing]
            remote(
                other, other, sib_s.at[0, mask], sib_s.at[1, mask], "expert", flipped(plane, mask)
            ).wait_recv()
        kv_turned = [kv_box[m].T for m in range(sharing)]
        for j in range(data):
            block_x = x_block(j)
            value = sum(
                jnp.dot(item, block_x, preferred_element_type=jnp.float32) for item in kv_turned
            )
            kv_part[j] = value.astype(jnp.bfloat16)
        kv_sum.begin(0)
        mixed_at = min(chunks, max(1, heads - 1)) if with_mix else chunks
        for k in range(mixed_at, chunks - 1):
            gather_mix(k)
        for c in range(chunks):
            reduce.advance(c, 0)
        if with_mix and mixed_at < chunks:
            gather_mix(chunks - 1)
        wo_sum.far(1)
        w_sum.near(0)
        for at in range(1, steps):
            for c in range(chunks):
                reduce.advance(c, at)
        router_stage(0)
        for c in range(chunks):
            reduce.result(c, dx_sum.at[:, pl.ds(c * width, width)])
        state = tok_ref[...].astype(jnp.float32)
        grad_normed = dx_sum[...]
        raw_grad, gain_term = norm_back(grad_normed, state, gain_ref[...])
        tok_out[...] += raw_grad
        vec[...] = jnp.zeros_like(vec)
        for c in range(chunks):
            cols = slice(c * width, (c + 1) * width)
            vec[c : c + 1, 0:width] = gain_term[:, cols]
            vec[chunks + c : chunks + c + 1, 0:width] = n2_ref[:, cols]
        vec[0:1, width : width + head] = gq_sum[...]
        vec[1:2, width : width + head] = gk_sum[...]
        for mask in range(1, group):
            vec_across(mask).start()
        sweeps = [(w_sum, h) for h in range(heads)] + [(kv_sum, 0)]
        if with_mix:
            for k in range(1, chunks):
                place_at = heads - mixed_at + 2 * k
                sweeps.insert(place_at if k < mixed_at else len(sweeps), (mix_sum, k))
        for at, (line, k) in enumerate(sweeps):
            if at:
                line.near(k)
                sweeps[at - 1][0].far(sweeps[at - 1][1])
                if at < steps + 3:
                    router_stage(at)
        sweeps[-1][0].far(sweeps[-1][1])
        for stage in range(max(1, min(len(sweeps), steps + 3)), steps + 3):
            router_stage(stage)
        all_sum = vec[...]
        for mask in range(1, group):
            vec_across(mask).wait_recv()
            all_sum = all_sum + vec_plane[mask]
        vec_half[...] = all_sum
        for step in range(1, data):
            vec_along(step).start()
        for k in range(2):
            wo_sum.result(k, wo_out.at[pl.ds(k * (wide // 2), wide // 2)])
        for h in range(heads):
            w_sum.result(h, summed)
            wq_out[:, h * head : (h + 1) * head] = summed[...].T
        kv_sum.result(0, wkv_out)
        if with_mix:
            for k in range(chunks):
                mix_sum.result(k, dx_sum.at[:, pl.ds(k * width, width)])
            layer_out[...] = (hid_ref[...] + dx_sum[...]).astype(jnp.bfloat16)
        for step in range(1, data):
            vec_along(step).wait_recv()
            all_sum = all_sum + vec_line[step]
        for c in range(chunks):
            cols = pl.ds(c * width, width)
            n1_out[:, cols] = all_sum[c : c + 1, 0:width]
            n2_out[:, cols] = all_sum[chunks + c : chunks + c + 1, 0:width]
        gq_out[...] = all_sum[0:1, width : width + head]
        gk_out[...] = all_sum[1:2, width : width + head]
        for mask in range(1, group):
            vec_across(mask).wait_send()
        for step in range(1, data):
            vec_along(step).wait_send()
            router_line(step).wait_send()
        router.finish(0)
        router_back.finish()
        for k in range(2):
            wo_sum.finish(k)
        for h in range(heads):
            w_sum.finish(h)
        kv_sum.finish(0)
        for mask in range(1, sharing):
            swap(mask).wait_send()
        for c in range(chunks):
            reduce.finish(c)
        if with_mix:
            for k in range(chunks):
                mix_sum.finish(k)
                if k:
                    exchange.finish(k)

    bf, fl = jnp.bfloat16, jnp.float32
    whole = pl.BlockSpec(memory_space=pltpu.VMEM)
    anywhere = pl.BlockSpec(memory_space=pl.ANY)
    mix_entries = entries if with_mix else 16
    mix_rows = rows if with_mix else 16
    mix_all = data * rows if with_mix else 16
    experts = router_sum.shape[0]
    share = model // group
    lines = whole_up(2 * chunks, 8)
    outs = [
        jax.ShapeDtypeStruct((rows, model), fl),
        jax.ShapeDtypeStruct((wide, cut), fl),
        jax.ShapeDtypeStruct((depth, wide), fl),
        jax.ShapeDtypeStruct((both, depth), fl),
        jax.ShapeDtypeStruct((1, head), fl),
        jax.ShapeDtypeStruct((1, head), fl),
        jax.ShapeDtypeStruct((1, model), fl),
        jax.ShapeDtypeStruct((1, model), fl),
        jax.ShapeDtypeStruct((experts, model), fl),
        jax.ShapeDtypeStruct((mix_rows, model), bf),
    ]
    return pl.pallas_call(
        kernel,
        out_shape=outs,
        in_specs=[whole]
        + [anywhere] * 10
        + [whole] * 5
        + [anywhere] * 2
        + [whole] * 2
        + [anywhere, whole if with_mix else anywhere, whole, anywhere]
        + [whole if with_mix else anywhere],
        out_specs=[whole] * len(outs),
        scratch_shapes=[
            vmem(out_blocks.shape, bf),
            vmem(x.shape, bf),
            vmem(w_q.shape, bf),
            vmem(w_kv.shape, bf),
            vmem(q_low.shape, bf),
            vmem(k_raw.shape, fl),
            vmem(k_low.shape, bf),
            vmem(v_low.shape, bf),
            vmem(lse.shape, fl),
            vmem(turned.shape if with_mix else (16, 128), bf),
            vmem((chunks, total, width), bf),
            vmem((head, total), fl),
            vmem((head, total), fl),
            vmem((total, wide), bf),
            vmem((total, head), fl),
            vmem((total, head), fl),
            vmem((sharing, total, both), bf),
            vmem((sharing, total, both), bf),
            vmem((2, total, head), fl),
            vmem((data, wide, cut), bf),
            vmem((data + 1, wide, cut), bf),
            vmem((heads, data, head, depth), bf),
            vmem((heads, data + 1, head, depth), bf),
            vmem((data, both, depth), bf),
            vmem((data + 1, both, depth), bf),
            vmem((chunks, group - 1, rows, width), bf),
            vmem((chunks, mix_entries, width), bf),
            vmem((chunks, mix_all, width), bf),
            vmem((chunks, data + 1, mix_rows, width), bf),
            vmem((head, depth), fl),
            vmem((rows, model), fl),
            vmem((lines, width + head), fl),
            vmem((group, lines, width + head), fl),
            vmem((lines, width + head), fl),
            vmem((data, lines, width + head), fl),
            vmem((experts, model), fl),
            vmem((group - 1, experts, share), fl),
            vmem((2, experts, share), fl),
            vmem((data, experts, share), fl),
            vmem((1, head), fl),
            vmem((1, head), fl),
            dma(12),
            dma(2),
            dma(chunks),
            dma(4, 2, data),
            dma(4, heads, data),
            dma(4, 1, data),
            dma(2, sharing),
            dma(2, chunks, group - 1),
            dma(2, chunks, group),
            dma(4, chunks, data),
            dma(2, group),
            dma(2, data),
            dma(2, 1, group - 1),
            dma(2, data),
            dma(2, 1, group),
            dma(2, pieces, group),
        ],
        compiler_params=pltpu.CompilerParams(
            collective_id=7, has_side_effects=True, vmem_limit_bytes=VMEM_LIMIT
        ),
    )(
        grad_branch, out_blocks, x, w_q, w_kv, q_raw, q_low, k_raw, k_low, v_low, lse, att,
        cos, sin, gain_q, gain_k, mixed, turned, tokens, gain, grad_hidden, hidden, norm2_sum, router_sum, first_mix,
    )


def rope_arrays(seq_len, head_dim):
    half = head_dim // 2
    frequency = ROPE_THETA ** (-(np.arange(half) * 2.0) / head_dim)
    angles = np.arange(seq_len)[:, None] * frequency[None, :]
    cos = np.concatenate([np.cos(angles), np.cos(angles)], axis=1).astype(np.float32)
    sin = np.concatenate([-np.sin(angles), np.sin(angles)], axis=1).astype(np.float32)
    return cos, sin


def row_scale(value):
    return lax.rsqrt(jnp.mean(value * value, axis=-1, keepdims=True) + NORM_EPS)


def half_turn(value):
    return pltpu.roll(value, value.shape[-1] // 2, value.ndim - 1)


def nt_dot(left, right):
    return lax.dot_general(
        left, right, (((1,), (1,)), ((), ())), preferred_element_type=jnp.float32
    )


def causal(start, rows, keys):
    at_row = lax.broadcasted_iota(jnp.int32, (rows, keys), 0) + start
    return lax.broadcasted_iota(jnp.int32, (rows, keys), 1) <= at_row


class Always:
    def __init__(self, order):
        self.order = order

    def __getitem__(self, at):
        return self.order


def front(
    tokens, gain, w_q, w_k, w_v, w_out, out_grad, slot_rows, cos, sin, gain_q, gain_k,
    gain2, router, hot, capacity, slots, seq_len,
):
    data, group = lax.axis_size("dp"), lax.axis_size("expert")
    rows, model = tokens.shape
    width = min(512, model)
    chunks = model // width
    depth, wide = w_q.shape
    cut = w_out.shape[1]
    part = w_k.shape[0]
    both = 2 * part
    head = gain_q.shape[1]
    sharing = head // part
    heads = wide // head
    total = group * rows
    block = min(256, seq_len)
    scale = head ** (-0.5)
    experts = router.shape[0]
    extra = whole_up(2 * experts, 128)
    entries = group * slots
    x_orders = bit_orders(group)
    x_orders = [x_orders[at % 2] for at in range(chunks)]
    b_orders = [Always(order[::-1]) for order in bit_orders(group)]
    steps = len(b_orders[0][0])
    halves = 2
    deep = depth // halves
    first_grad = 2 + halves
    first_out = first_grad + chunks - 1
    first_last = first_out + 1
    last = [item for item in halved(chunks, width, chunks - 1) if item[0] == chunks - 1]
    items = first_last + len(last)

    def kernel(
        tok_ref, gain_ref, wq_ref, wk_ref, wv_ref, wo_ref, og_ref, s_ref, cos_ref, sin_ref, gq_ref, gk_ref,
        gain2_ref, r_ref, hot_ref,
        x_any, wq_any, wkv_any, wo_any, g_any, sel_any, qr_any, ql_any, kr_any, kl_any, vl_any, lse_any,
        att_any, hidden, second, pair, probs,
        x_own, g_own, kv_own, x_all, wq_all, wkv_all, wo_all, g_all, s_all, picked, g_here, select,
        q_raw, q_low, k_raw, k_low, v_low, lse, att, acc, inbox,
        ps, ls, es, ks, bs, outs,
    ):
        place, plane = lax.axis_index("dp"), lax.axis_index("expert")
        member = plane % sharing
        state = tok_ref[...].astype(jnp.float32)
        normed = (state * row_scale(state) * gain_ref[...]).astype(jnp.bfloat16)
        mine = pl.ds(pl.multiple_of(place * rows, rows), rows)
        own_rows = pl.ds(pl.multiple_of(plane * rows, rows), rows)
        for c in range(chunks):
            x_own[c] = normed[:, c * width : (c + 1) * width]
            x_all[c, own_rows] = x_own[c]
            g_own[c] = og_ref[:, c * width : (c + 1) * width]
            g_all[c, mine] = g_own[c]
        kv_own[0:part] = wk_ref[...]
        kv_own[part:both] = wv_ref[...]
        wq_all[place] = wq_ref[...]
        wkv_all[member, place] = kv_own[...]
        wo_all[place] = wo_ref[...]
        s_all[place] = s_ref[...]
        greet()

        def token_rows(j):
            return pl.ds(pl.multiple_of(j * rows, rows), rows)

        def slot_rows_of(p):
            return pl.ds(pl.multiple_of(p * slots, slots), slots)

        gather = PlaneGather(
            lambda h: x_own.at[h], lambda h, j: x_all.at[h, token_rows(j)], ps, x_orders
        )

        def is_grad(k):
            return not isinstance(k, int) or first_grad <= k < first_out

        def own(k):
            if is_grad(k):
                return g_own.at[k - first_grad]
            if k == 0:
                return s_ref
            if k == 1:
                return kv_own
            if k < first_grad:
                return wq_ref.at[pl.ds((k - 2) * deep, deep)]
            if k >= first_last:
                return part_of(g_own, last[k - first_last], pl.ds(0, rows), width)
            return wo_ref

        def slot(k, j):
            if is_grad(k):
                return g_all.at[k - first_grad, token_rows(j)]
            if k == 0:
                return s_all.at[j]
            if k == 1:
                return wkv_all.at[member, j]
            if k < first_grad:
                return wq_all.at[j, pl.ds((k - 2) * deep, deep)]
            if k >= first_last:
                return part_of(g_all, last[k - first_last], token_rows(j), width)
            return wo_all.at[j]

        line = LineGather(own, slot, ls)
        def exchanged(ref):
            return lambda k, p: (
                part_of(ref, last[k - chunks + 1], slot_rows_of(p), width)
                if isinstance(k, int) and k >= chunks - 1
                else ref.at[k, slot_rows_of(p)]
            )

        exchange = PlaneExchange(exchanged(picked), exchanged(g_here), es)
        turns_of_grads = chunks - 1 + len(last)
        reduces = [
            PlaneReduce(lambda h, j: acc.at[h, j], lambda h, n: inbox.at[h, n], bs, order)
            for order in b_orders
        ]
        keeps = {}

        def keep(name, src, dst):
            keeps[name] = pltpu.make_async_copy(src, dst, outs.at[len(keeps)])
            keeps[name].start()

        def share(mask):
            return remote(
                wkv_all.at[member], wkv_all.at[member], ks.at[0, mask], ks.at[1, mask],
                "expert", flipped(plane, mask),
            )

        gather.start()
        for k in range(first_grad):
            line.start(k)
        moves = gather.moves()
        for s in range(1, data):
            line.step(0, s)
        wanted = lax.broadcasted_iota(jnp.int32, (slots, rows), 0).astype(jnp.float32)
        for j in range(data):
            for peer in range(group):
                row = s_all[j, pl.ds(pl.multiple_of(place * group, 8), group)][peer : peer + 1]
                row = jnp.where(row >= 0, row + j * capacity, -1.0)
                select[pl.ds(peer * slots, slots), pl.ds(j * rows, rows)] = jnp.where(
                    wanted == row, 1.0, 0.0
                ).astype(jnp.bfloat16)
        for k in range(first_grad, min(first_grad + 2, first_out)):
            line.start(k)
        taken = 0
        turns = [(k, s) for k in range(1, first_grad) for s in range(1, data)]
        for at, (k, s) in enumerate(turns):
            until = len(moves) * (at + 1) // len(turns)
            for move in moves[taken:until]:
                gather.move(*move)
            taken = until
            line.step(k, s)
            if k == 1 and s == data - 1:
                for mask in range(1, sharing):
                    share(mask).start()
        for k in range(first_grad + 2, first_out):
            line.start(k)
        for mask in range(1, sharing):
            other = wkv_all.at[flipped(plane, mask) % sharing]
            remote(
                other, other, ks.at[0, mask], ks.at[1, mask], "expert", flipped(plane, mask)
            ).wait_recv()
        keep("select", select, sel_any)
        keep("x", x_all, x_any)
        keep("wq", wq_all, wq_any)
        keep("wkv", wkv_all, wkv_any)

        def x_block(rows_here, j):
            first = j * depth
            inner = first % width
            return x_all[first // width, rows_here, inner : inner + depth]

        def project(at, carry):
            here = pl.ds(pl.multiple_of(at * block, block), block)
            table = pl.ds(pl.multiple_of((at * block) % seq_len, block), block)
            cos_here, sin_here = cos_ref[table], sin_ref[table]
            blocks = [x_block(here, j) for j in range(data)]
            raw = sum(
                jnp.dot(blocks[j], wq_all[j], preferred_element_type=jnp.float32)
                for j in range(data)
            )
            q_raw[here] = raw
            for h in range(heads):
                one = raw[:, h * head : (h + 1) * head]
                one = one * row_scale(one) * gq_ref[...]
                turned = one * cos_here + half_turn(one) * sin_here
                q_low[here, h * head : (h + 1) * head] = turned.astype(jnp.bfloat16)
            kv = [sum(nt_dot(blocks[j], wkv_all[m, j]) for j in range(data)) for m in range(sharing)]
            raw = jnp.concatenate([item[:, :part] for item in kv], axis=1)
            k_raw[here] = raw
            one = raw * row_scale(raw) * gk_ref[...]
            k_low[here] = (one * cos_here + half_turn(one) * sin_here).astype(jnp.bfloat16)
            v_low[here] = jnp.concatenate([item[:, part:] for item in kv], axis=1).astype(
                jnp.bfloat16
            )
            return carry

        lax.fori_loop(0, total // block, project, 0)
        keep("q_raw", q_raw, qr_any)
        keep("q_low", q_low, ql_any)
        keep("k_raw", k_raw, kr_any)
        keep("k_low", k_low, kl_any)
        keep("v_low", v_low, vl_any)
        lane = lax.broadcasted_iota(jnp.int32, (block, head), 1)
        below = causal(0, block, block)
        lse[...] = jnp.zeros_like(lse)

        def send_grads(c):
            picked[c] = jnp.dot(
                select[...], g_all[c], preferred_element_type=jnp.float32
            ).astype(jnp.bfloat16)
            exchange.start(c)
            exchange.keep(c)

        def attend(h, carry):
            cols = pl.ds(pl.multiple_of(h * head, head), head)
            count = 0
            for seq in range(total // seq_len):
                base = seq * seq_len
                for at in range(seq_len // block):
                    here = pl.ds(base + at * block, block)
                    query = q_low[here, cols]
                    tiles = []
                    if at:
                        tiles.append(pl.ds(base, at * block))
                    tiles.append(here)
                    scores = [nt_dot(query, k_low[tile]) for tile in tiles]
                    scores[-1] = jnp.where(below, scores[-1], -jnp.inf)
                    top = jnp.max(scores[-1], axis=-1, keepdims=True)
                    if at:
                        top = jnp.maximum(top, jnp.max(scores[0], axis=-1, keepdims=True))
                    raised = [jnp.exp2((score - top) * (scale * LOG2_E)) for score in scores]
                    norm = sum(jnp.sum(item, axis=-1, keepdims=True) for item in raised)
                    inverse = 1.0 / norm
                    att[here, cols] = sum(
                        jnp.dot(
                            (item * inverse).astype(jnp.bfloat16),
                            v_low[tile],
                            preferred_element_type=jnp.float32,
                        )
                        for item, tile in zip(raised, tiles)
                    ).astype(jnp.bfloat16)
                    lse[here] = jnp.where(lane == h, top * scale + jnp.log(norm), lse[here])
                    count += 1
                    if count < data:

                        @pl.when(h < chunks - 1)
                        def _():
                            line.step(first_grad + h, count)

            @pl.when(h < chunks - 1)
            def _():
                for s in range(count + 1, data):
                    line.step(first_grad + h, s)
                send_grads(h)

            @pl.when(h == 0)
            def _():
                line.start(first_out)

            return carry

        lax.fori_loop(0, heads, attend, 0)
        keep("lse", lse, lse_any)
        keep("att", att, att_any)
        for c in range(heads, chunks - 1):
            for s in range(1, data):
                line.step(first_grad + c, s)
            send_grads(c)
        for k in range(first_last, items):
            line.start(k)

        def send_last(n):
            c, at, wide = last[n]
            picked[c, :, at : at + wide] = jnp.dot(
                select[...], g_all[c, :, at : at + wide], preferred_element_type=jnp.float32
            ).astype(jnp.bfloat16)
            exchange.start(chunks - 1 + n)
            exchange.keep(chunks - 1 + n)

        tail = []
        for n in range(len(last)):
            tail += [(n, s) for s in range(1, data)]

        def arrivals(s):
            if s == 0:
                return [(place, place >= 0, reduces[0])]
            return [
                (place - s, place >= s, reduces[(s + 1) % 2]),
                (place + s, place + s < data, reduces[s % 2]),
            ]

        def each(s, act):
            for j, present, reduce in arrivals(s):

                @pl.when(present)
                def _():
                    act(j, reduce)

        def project_out(j, reduce):
            acc[j] = (
                jnp.dot(att[...], wo_all[j], preferred_element_type=jnp.float32)
                .astype(jnp.bfloat16)
                .reshape(group, rows, cut)
            )
            reduce.start(j)

        for turn in range(data + steps):
            if turn < data:
                if turn:
                    line.step(first_out, turn)
                each(turn, project_out)
            for at in range(steps):
                if 0 <= turn - 1 - at < data:
                    each(turn - 1 - at, lambda j, reduce: reduce.advance(j, at))
            if turn >= data - 1:
                count = -(-len(tail) // (data + steps - turn))
                for n, s in tail[:count]:
                    line.step(first_last + n, s)
                    if s == data - 1:
                        send_last(n)
                tail = tail[count:]
        keep("wo", wo_all, wo_any)

        def branch_piece(j, reduce):
            reduce.result(j, hidden.at[:, pl.ds(pl.multiple_of(j * cut, cut), cut)])

        for s in range(data):
            each(s, branch_piece)
        summed = hidden[...] + tok_ref[...].astype(jnp.float32)
        hidden[...] = summed
        low = (summed * row_scale(summed) * gain2_ref[...]).astype(jnp.bfloat16)
        for c in range(chunks):
            second[c] = low[:, c * width : (c + 1) * width]
        logits = nt_dot(low, r_ref[...])
        masked = jnp.where(hot_ref[...] > 0, logits, -jnp.inf)
        raised = jnp.exp(masked - jnp.max(masked, axis=-1, keepdims=True))
        gate = raised / jnp.sum(raised, axis=-1, keepdims=True)
        probs[...] = gate
        top = gate.astype(jnp.bfloat16).astype(jnp.float32)
        parts = [top, gate - top]
        if extra > 2 * experts:
            parts.append(jnp.zeros((rows, extra - 2 * experts), jnp.float32))
        pair[...] = jnp.concatenate(parts, axis=1).astype(jnp.bfloat16)
        for k in range(turns_of_grads):
            exchange.wait(k)
        keep("g", g_here, g_any)
        for k in range(items):
            line.finish(k)
        gather.finish()
        for mask in range(1, sharing):
            share(mask).wait_send()
        for k in range(turns_of_grads):
            exchange.finish(k)
        for s in range(data):
            each(s, lambda j, reduce: reduce.finish(j))
        for copy in keeps.values():
            copy.wait()

    bf, fl = jnp.bfloat16, jnp.float32
    whole = pl.BlockSpec(memory_space=pltpu.VMEM)
    anywhere = pl.BlockSpec(memory_space=pl.ANY)

    def shape(*dims, dtype=bf):
        return jax.ShapeDtypeStruct(dims, dtype)

    kept = [
        shape(chunks, total, width),
        shape(data, depth, wide),
        shape(sharing, data, both, depth),
        shape(data, wide, cut),
        shape(chunks, entries, width),
        shape(entries, data * rows),
        shape(total, wide, dtype=fl),
        shape(total, wide),
        shape(total, head, dtype=fl),
        shape(total, head),
        shape(total, head),
        shape(total, head, dtype=fl),
        shape(total, wide),
    ]
    small = [
        shape(rows, model, dtype=fl),
        shape(chunks, rows, width),
        shape(rows, extra),
        shape(rows, experts, dtype=fl),
    ]
    return pl.pallas_call(
        kernel,
        out_shape=kept + small,
        in_specs=[whole] * 15,
        out_specs=[anywhere] * len(kept) + [whole] * len(small),
        scratch_shapes=[
            vmem((chunks, rows, width), bf),
            vmem((chunks, rows, width), bf),
            vmem((both, depth), bf),
            vmem((chunks, total, width), bf),
            vmem((data, depth, wide), bf),
            vmem((sharing, data, both, depth), bf),
            vmem((data, wide, cut), bf),
            vmem((chunks, data * rows, width), bf),
            vmem((data, experts, rows), fl),
            vmem((chunks, entries, width), bf),
            vmem((chunks, entries, width), bf),
            vmem((entries, data * rows), bf),
            vmem((total, wide), fl),
            vmem((total, wide), bf),
            vmem((total, head), fl),
            vmem((total, head), bf),
            vmem((total, head), bf),
            vmem((total, head), fl),
            vmem((total, wide), bf),
            vmem((data, group, rows, cut), bf),
            vmem((data, group - 1, rows, cut), bf),
            dma(2, chunks, group),
            dma(4, items, data - 1),
            dma(2, chunks - 1 + len(last), group),
            dma(2, sharing),
            dma(2, data, group - 1),
            dma(len(kept)),
        ],
        compiler_params=pltpu.CompilerParams(
            collective_id=1, has_side_effects=True, vmem_limit_bytes=VMEM_LIMIT
        ),
    )(
        tokens, gain, w_q, w_k, w_v, w_out, out_grad, slot_rows, cos, sin, gain_q, gain_k,
        gain2, router, hot,
    )


def local(
    tokens,
    norm1_gain,
    w_query,
    key_weight,
    value_weight,
    w_out,
    query_gain,
    key_gain,
    norm2_gain,
    w_router,
    w_gate,
    w_up,
    w_down,
    routes,
    out_grad,
):
    data_count = lax.axis_size("dp")
    group_count = lax.axis_size("expert")
    group_index = lax.axis_index("expert")
    local_rows = tokens.shape[0]
    model_width = tokens.shape[1]
    head_dim = query_gain.shape[0]
    heads_here = w_query.shape[1] // head_dim
    top_count = routes.shape[1]
    expert_total = data_count * group_count
    capacity = max(2, (local_rows * top_count * 9 + 8 * expert_total - 1) // (8 * expert_total))
    data_index = lax.axis_index("dp")
    own_expert = data_index * group_count + group_index
    expert_ids = jnp.arange(expert_total)
    hot = jnp.any(routes[:, :, None] == expert_ids[None, None, :], axis=1)
    earlier = (jnp.arange(local_rows)[:, None] > jnp.arange(local_rows)[None, :]).astype(jnp.bfloat16)
    rank = jnp.dot(earlier, hot.astype(jnp.bfloat16), preferred_element_type=jnp.float32)
    slot_rows = jnp.where(hot, rank, -1.0).T
    slots = whole_up(data_count * capacity, 16)
    width_k = key_weight.shape[1]
    all_rows = group_count * local_rows
    seq_len = min(SEQ_LEN, all_rows)
    router = w_router.T
    cos_rows, sine_rows = [jnp.asarray(table) for table in rope_arrays(seq_len, head_dim)]
    (
        gathered, q_blocks, kv_blocks, out_blocks, grads_here, select, query_raw, queries, key_raw,
        keys_low, values_low, log_sum, attended, hidden, second, pair, gate_probs,
    ) = front(
        tokens, norm1_gain[None], w_query, key_weight.T, value_weight.T, w_out, out_grad, slot_rows,
        cos_rows, sine_rows, query_gain[None], key_gain[None], norm2_gain[None], router,
        hot.astype(jnp.float32), capacity, slots, seq_len,
    )
    q_cols = q_blocks.reshape(model_width, -1)
    with_mix = all_rows <= group_count * slots
    (
        arrived, grad_arrived, low_rows, mixed, grad_hidden, grad_branch, grad_norm2, grad_router,
        turned, first_mix,
    ) = expert_layer(
        second, pair, gate_probs, hidden, out_grad, norm2_gain[None], router, select, grads_here,
        w_gate[0], w_up[0], w_down[0], out_blocks.shape[2], with_mix,
    )
    (
        grad_tokens, grad_wo, grad_wq, grad_wkv, grad_query_gain, grad_key_gain, grad_norm1,
        grad_norm2, grad_router, output,
    ) = attention_backward(
        grad_branch, out_blocks, gathered, q_cols, kv_blocks, query_raw, queries, key_raw, keys_low,
        values_low, log_sum, attended, cos_rows, sine_rows, query_gain[None], key_gain[None],
        mixed, turned, tokens, norm1_gain[None], grad_hidden, hidden, grad_norm2, grad_router, first_mix,
        seq_len, with_mix,
    )
    if not with_mix:
        output = (hidden + combine(mixed, select, slots, 5)).astype(jnp.bfloat16)
    (
        grad_gate_w, grad_up_w, grad_down, output, grad_tokens, grad_wq, grad_wo, grad_router,
        grad_wk, grad_wv,
    ) = expert_weight_grads(
        arrived, grad_arrived, low_rows, [output, grad_tokens, grad_wq, grad_wo, grad_router],
        grad_wkv,
    )
    return (
        output,
        grad_tokens,
        grad_norm1[0],
        grad_wq,
        grad_wk.T,
        grad_wv.T,
        grad_wo,
        grad_query_gain[0],
        grad_key_gain[0],
        grad_norm2[0],
        grad_router.T,
        grad_gate_w,
        grad_up_w,
        grad_down,
    )


def solution(mesh):
    placed = (
        P(("dp", "expert"), None),
        P(),
        P("dp", "expert"),
        P("dp", "expert"),
        P("dp", "expert"),
        P("expert", "dp"),
        P(),
        P(),
        P(),
        P(),
        P(("dp", "expert"), None, None),
        P(("dp", "expert"), None, None),
        P(("dp", "expert"), None, None),
        P(("dp", "expert"), None),
        P(("dp", "expert"), None),
    )
    return jax.shard_map(
        local,
        mesh=mesh,
        in_specs=placed,
        out_specs=(
            P(("dp", "expert"), None),
            P(("dp", "expert"), None),
            P(),
            P("dp", "expert"),
            P("dp", "expert"),
            P("dp", "expert"),
            P("expert", "dp"),
            P(),
            P(),
            P(),
            P(),
            P(("dp", "expert"), None, None),
            P(("dp", "expert"), None, None),
            P(("dp", "expert"), None, None),
        ),
        check_vma=False,
    )
```

time: 1280 us -> 500 us (0.39)
  waiting for transfers between devices: 565 us -> 0 us
  Pallas kernels: 0 us -> 487 us
  blocking collectives: 314 us -> 0 us
  matrix products: 138 us -> 0.76 us
  local copies, waits for them, and re-layouts: 136 us -> 2.97 us
  other arithmetic: 90.7 us -> 0.71 us
  between operations: 15.3 us -> 1.16 us
    pallas_call x0 -> x4, Pallas kernels: none -> 487 us  [the longest x1 163 us: expert_layer(): pl.pallas_call(kernel, out_shape=outs, in_specs=[whole] * 8 + [anywhere]...]
    all_to_all x2 -> x0, blocking collectives: 241 us -> none  [move_rows(): lax.all_to_all(buffer, ('dp', 'expert'), split_axis=0, concat_axis=0, til...]
    all_to_all x2 -> x0, waiting for transfers between devices: 228 us -> none  [move_rows(): lax.all_to_all(buffer, ('dp', 'expert'), split_axis=0, concat_axis=0, til...]
    reduce_scatter x6 -> x0, waiting for transfers between devices: 166 us -> none  [the longest x1 59.5 us: local(): lax.psum_scatter(jnp.dot(attended, o_rows, preferred_element_type=jnp.flo...]
    dot_general x39 -> x1, matrix products: 138 us -> 0.76 us  [local(): jnp.dot(earlier, hot.astype(jnp.bfloat16), preferred_element_type=jnp.flo...]
    psum x1 -> x0, waiting for transfers between devices: 85.2 us -> none  [local(): lax.psum((grad_norm1, grad_query_gain, grad_key_gain, grad_norm2, grad_ro...]
    all_gather x4 -> x0, waiting for transfers between devices: 84.6 us -> none  [the longest x1 35.6 us: local(): lax.all_gather(w_query, 'dp', axis=0, tiled=True)]
    reshape x10 -> x0, local copies, waits for them, and re-layouts: 63.7 us -> none  [the longest x1 7.59 us: local(): move_rows(grad_rows.reshape(expert_total, capacity, model_width))]
  transfers between devices with their start and end apart: 17 -> 0, of which waited for: 11 -> 0; matrix products, arithmetic and copies ran while one was open for 13% -> 0% of each run, Pallas kernels for 0% -> 0%
where the time goes in v1:
time: 500 us; the launch traced here: 493 us
  Pallas kernels  487 us (97%)
    pallas_call x1, Pallas kernels, expert_layer(): pl.pallas_call(kernel, out_shape=outs, in_specs=[whole] * 8 + [anywhere]...  163 us
    pallas_call x1, Pallas kernels, attention_backward(): pl.pallas_call(kernel, out_shape=outs, in_specs=[whole] + [anywhere] * 10...  153 us
    pallas_call x1, Pallas kernels, front(): pl.pallas_call(kernel, out_shape=kept + small, in_specs=[whole] * 15, out...  151 us
    pallas_call x1, Pallas kernels, expert_weight_grads(): pl.pallas_call(kernel, grid=(chunks,), out_shape=[jax.ShapeDtypeStruct((1...  20.3 us

profile of v1, /device:TPU:0, one launch (start us, length us, event | category | flops | bytes accessed | tf_op | source)
XLA Modules:
  0.0 492.6 jit_solution(14540085388676365433)
XLA Ops:
  0.6 0.7 fusion
  1.4 0.8 convolution_select_fusion.s_ref
  2.1 0.7 copy.35.hot_ref
  2.9 150.9 %shard_map.272 = (bf16[4,1024,512]{2,1,0:T(8,128)(2,1)}, bf16[4,512,512]{2,1,0:T(8,128)(2,1)}, bf16[2,4,128,512]{3,2,1,0:T(8,128)(2,1)}, bf16[4,512,512]{2,1,0:T...) custom-call(bf16[128,2048]{1,0:T(8,128)(2,1)} %tok_ref.3, ...), custom_call_target="tpu_custom_call" | custom-call | tf_op jit(solution)/shard_map/pallas_call | solution.py:1908
  153.8 162.6 %shard_map.273 = (bf16[4,1152,512]{2,1,0:T(8,128)(2,1)}, bf16[4,1152,512]{2,1,0:T(8,128)(2,1)}, bf16[3,1152,768]{2,1,0:T(8,128)(2,1)}, bf16[4,1152,512]{2,1,0:T(...) custom-call(bf16[4,128,512]{2,1,0:T(8,128)(2,1)} %get-tuple-element., ...), custom_call_target="tpu_custom_call" | custom-call | tf_op jit(solution)/shard_map/pallas_call | solution.py:796
  316.4 153.2 %shard_map.274 = (f32[128,2048]{1,0:T(8,128)}, f32[512,512]{1,0:T(8,128)}, f32[512,512]{1,0:T(8,128)}, f32[128,512]{1,0:T(8,128)}, f32[1,128]{1,0:T(1,128)}, /*i...) custom-call(bf16[4,128,512]{2,1,0:T(8,128)(2,1)} %get-tuple-element., ...), custom_call_target="tpu_custom_call" | custom-call | tf_op jit(solution)/shard_map/pallas_call | solution.py:1408
  469.6 0.0 copy-start.1
  469.6 0.0 copy-start.3
  469.6 0.0 copy-start.2
  469.6 0.0 copy-start
  469.6 20.3 %shard_map.275 = (f32[1,2048,768]{2,1,0:T(8,128)}, f32[1,2048,768]{2,1,0:T(8,128)}, f32[1,768,2048]{2,1,0:T(8,128)}, bf16[128,2048]{1,0:T(8,128)(2,1)}, f32[128,...) custom-call(bf16[4,1152,512]{2,1,0:T(8,128)(2,1)} %get-tuple-element, ...), custom_call_target="tpu_custom_call" | custom-call | tf_op jit(solution)/shard_map/pallas_call | solution.py:876
  489.9 0.0 copy-done.1
  489.9 0.6 copy.40
  490.5 0.0 copy-done.3
  490.5 0.5 copy.41
  491.1 0.0 copy-done.2
  491.1 0.5 copy.42
  491.6 0.0 copy-done
  491.6 0.6 copy.43
  (1 shorter events, 0.0 us)
Async XLA Ops:
  469.6 20.3 %copy-start.1 = (f32[1,2048]{1,0:T(1,128)S(1)}, f32[1,2048]{1,0:T(1,128)}, u32[]{:S(2)}) copy-start(f32[1,2048]{1,0:T(1,128)} %get-tuple-element.96) | copy-start | bytes 24580
  469.6 20.9 %copy-start.3 = (f32[1,128]{1,0:T(1,128)S(1)}, f32[1,128]{1,0:T(1,128)}, u32[]{:S(2)}) copy-start(f32[1,128]{1,0:T(1,128)} %get-tuple-element.101) | copy-start | bytes 1540
  469.6 21.5 %copy-start.2 = (f32[1,128]{1,0:T(1,128)S(1)}, f32[1,128]{1,0:T(1,128)}, u32[]{:S(2)}) copy-start(f32[1,128]{1,0:T(1,128)} %get-tuple-element.102) | copy-start | bytes 1540
  469.6 22.0 %copy-start = (f32[1,2048]{1,0:T(1,128)S(1)}, f32[1,2048]{1,0:T(1,128)}, u32[]{:S(2)}) copy-start(f32[1,2048]{1,0:T(1,128)} %get-tuple-element.103) | copy-start | bytes 24580

commit v2 on v1

--- a/solution.py
+++ b/solution.py
@@ -499,11 +499,11 @@
 
     def kernel(
         sec_ref, pair_ref, prob_ref, hid_ref, g_ref, gain_ref, r_ref, select, gh_any, wg_any, wu_any, wd_any,
-        x_any, s_any, h_any, v_any, grad_hidden, branch_any, norm_sum, router_sum, turned_any, mix_out,
+        d_any, s_any, a_any, v_any, grad_hidden, branch_any, norm_sum, router_sum, turned_any, mix_out,
         x_all, pair_all, picked_pair, pair_here, rows_out, pair_out, back, pair_back,
         inbox, pair_box, summed, pair_sum, turned, low, wg, wu, wd,
-        x_here, g_stage, s_stage, v_stage, h_stage,
-        mix_back, loads, g_load, stores, keeps, ls, es, ls2, es2, es3,
+        x_here, g_stage, s_stage, v_stage, a_stage, grad_h, d_stage,
+        mix_back, loads, g_load, stores, keeps, d_s, ls, es, ls2, es2, es3,
     ):
         place, plane = lax.axis_index("dp"), lax.axis_index("expert")
         own = place * group + plane
@@ -535,7 +535,7 @@
             return [
                 pltpu.make_async_copy(s_stage.at[slot], s_any.at[:, here], stores.at[slot, 0]),
                 pltpu.make_async_copy(v_stage.at[slot], v_any.at[:, here], stores.at[slot, 1]),
-                pltpu.make_async_copy(h_stage.at[slot], h_any.at[:, here], stores.at[slot, 2]),
+                pltpu.make_async_copy(a_stage.at[slot], a_any.at[here], stores.at[slot, 2]),
             ]
 
         load_grads(0).start()
@@ -600,8 +600,6 @@
             exchange.wait(k)
         for k in range(len(came) + 1):
             exchange.finish(k)
-        keep_rows = pltpu.make_async_copy(x_here, x_any, keeps.at[0])
-        keep_rows.start()
 
         give_back = PlaneExchange(
             pick(sent, rows_out, pair_out), pick(sent, back, pair_back), es2
@@ -637,7 +635,7 @@
             sigmoid = jax.nn.sigmoid(gate_h)
             silu = gate_h * sigmoid
             active = (silu * up_h).astype(jnp.bfloat16)
-            h_stage[slot, 0] = active
+            a_stage[slot] = active
             grad_active = jnp.zeros((block, hidden_units), jnp.float32)
             slot_gate = jnp.zeros((block, 1), jnp.float32)
             for c in range(chunks):
@@ -653,8 +651,8 @@
             grad_gate_h = grad_active * up_h * sigmoid * (1.0 + gate_h * (1.0 - sigmoid))
             grad_gate_h = grad_gate_h.astype(jnp.bfloat16)
             grad_up_h = (grad_active * silu).astype(jnp.bfloat16)
-            h_stage[slot, 1] = grad_gate_h
-            h_stage[slot, 2] = grad_up_h
+            grad_h[0, here] = grad_gate_h
+            grad_h[1, here] = grad_up_h
             for store in store_block(step):
                 store.start()
             top = slot_gate.astype(jnp.bfloat16).astype(jnp.float32)
@@ -678,7 +676,21 @@
             return carry
 
         lax.fori_loop(0, pairs, run_block, 0)
-        keep_rows.wait()
+        def store_grads(c, side):
+            return pltpu.make_async_copy(
+                d_stage.at[side], d_any.at[side, pl.ds(c * width, width)], d_s.at[side]
+            )
+
+        def weight_grads(c):
+            x = x_here[c].T
+            for side in range(2):
+                if c:
+                    store_grads(c - 1, side).wait()
+                d_stage[side] = jnp.dot(
+                    x, grad_h[side], preferred_element_type=jnp.float32
+                ).astype(jnp.bfloat16)
+                store_grads(c, side).start()
+
         for step in range(max(0, pairs - 2), pairs):
             for store in store_block(step):
                 store.wait()
@@ -727,6 +739,8 @@
                 sums.near(order[at - 1])
             if at >= 2:
                 sums.far(order[at - 2])
+            if at < chunks:
+                weight_grads(at)
         if with_mix:
             mix.start(0)
             own_mix.start()
@@ -772,6 +786,8 @@
                 turned[...], mix_back[...], preferred_element_type=jnp.float32
             ).astype(jnp.bfloat16)
             mix.finish(0)
+        for side in range(2):
+            store_grads(chunks - 1, side).wait()
         keep_turned.wait()
         keep_low.wait()
         for k in range(len(sent) + 1):
@@ -782,9 +798,9 @@
     whole = pl.BlockSpec(memory_space=pltpu.VMEM)
     anywhere = pl.BlockSpec(memory_space=pl.ANY)
     outs = [
+        jax.ShapeDtypeStruct((2, model, hidden_units), bf),
         jax.ShapeDtypeStruct((chunks, entries, width), bf),
-        jax.ShapeDtypeStruct((chunks, entries, width), bf),
-        jax.ShapeDtypeStruct((3, entries, hidden_units), bf),
+        jax.ShapeDtypeStruct((entries, hidden_units), bf),
         jax.ShapeDtypeStruct((chunks, entries, width), bf),
         jax.ShapeDtypeStruct((rows, model), fl),
         jax.ShapeDtypeStruct((pieces, rows, cut), bf),
@@ -820,12 +836,15 @@
             vmem((2, chunks, block, width), bf),
             vmem((2, chunks, block, width), bf),
             vmem((2, chunks, block, width), bf),
-            vmem((2, 3, block, hidden_units), bf),
+            vmem((2, block, hidden_units), bf),
+            vmem((2, entries, hidden_units), bf),
+            vmem((2, width, hidden_units), bf),
             vmem((entries if with_mix else 16, width), bf),
             dma(3),
             dma(2),
             dma(2, 3),
             dma(4),
+            dma(2),
             dma(4, len(came) + 1, data - 1),
             dma(2, len(came) + 1, group),
             dma(4, len(sent) + 1, data),
@@ -842,13 +861,13 @@
     return results
 
 
-def expert_weight_grads(arrived, grad_arrived, low_rows, others, kv):
-    chunks, entries, width = arrived.shape
-    hidden_units = low_rows.shape[2]
+def expert_weight_grads(grad_h, grad_arrived, act, others, kv, small):
+    chunks, entries, width = grad_arrived.shape
+    hidden_units = act.shape[1]
     part = kv.shape[0] // 2
-    passed = len(others) + 2
-
-    def kernel(x_ref, s_ref, low_ref, *refs):
+    passed = len(others) + 2 + len(small)
+
+    def kernel(h_ref, s_ref, act_ref, *refs):
         sources = refs[:passed]
         gate_out, up_out, down_out = refs[passed : passed + 3]
         targets = refs[passed + 3 : 2 * passed + 3]
@@ -856,16 +875,14 @@
 
         @pl.when(pl.program_id(0) == 0)
         def _():
-            turned[...] = low_ref[0].T
+            turned[...] = act_ref[...].T
 
         for source, target in zip(sources, targets):
             target[...] = source[...]
-        x = x_ref[0].T
-        gate_out[0] = jnp.dot(x, low_ref[1], preferred_element_type=jnp.float32)
-        up_out[0] = jnp.dot(x, low_ref[2], preferred_element_type=jnp.float32)
+        gate_out[0] = h_ref[0].astype(jnp.float32)
+        up_out[0] = h_ref[1].astype(jnp.float32)
         down_out[0] = jnp.dot(turned[...], s_ref[0], preferred_element_type=jnp.float32)
 
-    rows = pl.BlockSpec((1, entries, width), lambda c: (c, 0, 0))
     tall = pl.BlockSpec((1, width, hidden_units), lambda c: (0, c, 0))
 
     def slab(lines, item, first=0):
@@ -873,6 +890,7 @@
 
     slabs = [slab(item.shape[0], item) for item in others]
     half = slab(part, kv)
+    whole = [pl.BlockSpec(item.shape, lambda c: (0, 0)) for item in small]
     return pl.pallas_call(
         kernel,
         grid=(chunks,),
@@ -882,16 +900,23 @@
             jax.ShapeDtypeStruct((1, hidden_units, chunks * width), jnp.float32),
         ]
         + [jax.ShapeDtypeStruct(item.shape, item.dtype) for item in others]
-        + [jax.ShapeDtypeStruct((part, kv.shape[1]), kv.dtype)] * 2,
-        in_specs=[rows, rows, pl.BlockSpec((3, entries, hidden_units), lambda c: (0, 0, 0))]
+        + [jax.ShapeDtypeStruct((part, kv.shape[1]), kv.dtype)] * 2
+        + [jax.ShapeDtypeStruct(item.shape, item.dtype) for item in small],
+        in_specs=[
+            pl.BlockSpec((2, width, hidden_units), lambda c: (0, c, 0)),
+            pl.BlockSpec((1, entries, width), lambda c: (c, 0, 0)),
+            pl.BlockSpec((entries, hidden_units), lambda c: (0, 0)),
+        ]
         + slabs
-        + [half, slab(part, kv, chunks)],
+        + [half, slab(part, kv, chunks)]
+        + whole,
         out_specs=[tall, tall, pl.BlockSpec((1, hidden_units, width), lambda c: (0, 0, c))]
         + slabs
-        + [half, half],
+        + [half, half]
+        + whole,
         scratch_shapes=[vmem((hidden_units, entries), jnp.bfloat16)],
         compiler_params=pltpu.CompilerParams(vmem_limit_bytes=VMEM_LIMIT),
-    )(arrived, grad_arrived, low_rows, *others, kv, kv)
+    )(grad_h, grad_arrived, act, *others, kv, kv, *small)
 
 
 def attention_backward(
@@ -1328,6 +1353,14 @@
                 place_at = heads - mixed_at + 2 * k
                 sweeps.insert(place_at if k < mixed_at else len(sweeps), (mix_sum, k))
         for at, (line, k) in enumerate(sweeps):
+            if at == 2:
+                all_sum = vec[...]
+                for mask in range(1, group):
+                    vec_across(mask).wait_recv()
+                    all_sum = all_sum + vec_plane[mask]
+                vec_half[...] = all_sum
+                for step in range(1, data):
+                    vec_along(step).start()
             if at:
                 line.near(k)
                 sweeps[at - 1][0].far(sweeps[at - 1][1])
@@ -1336,13 +1369,6 @@
         sweeps[-1][0].far(sweeps[-1][1])
         for stage in range(max(1, min(len(sweeps), steps + 3)), steps + 3):
             router_stage(stage)
-        all_sum = vec[...]
-        for mask in range(1, group):
-            vec_across(mask).wait_recv()
-            all_sum = all_sum + vec_plane[mask]
-        vec_half[...] = all_sum
-        for step in range(1, data):
-            vec_along(step).start()
         for k in range(2):
             wo_sum.result(k, wo_out.at[pl.ds(k * (wide // 2), wide // 2)])
         for h in range(heads):
@@ -1353,13 +1379,15 @@
             for k in range(chunks):
                 mix_sum.result(k, dx_sum.at[:, pl.ds(k * width, width)])
             layer_out[...] = (hid_ref[...] + dx_sum[...]).astype(jnp.bfloat16)
+        all_sum = vec_half[...]
         for step in range(1, data):
             vec_along(step).wait_recv()
             all_sum = all_sum + vec_line[step]
         for c in range(chunks):
-            cols = pl.ds(c * width, width)
-            n1_out[:, cols] = all_sum[c : c + 1, 0:width]
-            n2_out[:, cols] = all_sum[chunks + c : chunks + c + 1, 0:width]
+            for q in range(width // 128):
+                at, cols = c * (width // 128) + q, slice(q * 128, (q + 1) * 128)
+                n1_out[at : at + 1] = all_sum[c : c + 1, cols]
+                n2_out[at : at + 1] = all_sum[chunks + c : chunks + c + 1, cols]
         gq_out[...] = all_sum[0:1, width : width + head]
         gk_out[...] = all_sum[1:2, width : width + head]
         for mask in range(1, group):
@@ -1400,8 +1428,8 @@
         jax.ShapeDtypeStruct((both, depth), fl),
         jax.ShapeDtypeStruct((1, head), fl),
         jax.ShapeDtypeStruct((1, head), fl),
-        jax.ShapeDtypeStruct((1, model), fl),
-        jax.ShapeDtypeStruct((1, model), fl),
+        jax.ShapeDtypeStruct((model // 128, 128), fl),
+        jax.ShapeDtypeStruct((model // 128, 128), fl),
         jax.ShapeDtypeStruct((experts, model), fl),
         jax.ShapeDtypeStruct((mix_rows, model), bf),
     ]
@@ -1999,7 +2027,7 @@
     q_cols = q_blocks.reshape(model_width, -1)
     with_mix = all_rows <= group_count * slots
     (
-        arrived, grad_arrived, low_rows, mixed, grad_hidden, grad_branch, grad_norm2, grad_router,
+        grad_h, grad_arrived, act, mixed, grad_hidden, grad_branch, grad_norm2, grad_router,
         turned, first_mix,
     ) = expert_layer(
         second, pair, gate_probs, hidden, out_grad, norm2_gain[None], router, select, grads_here,
@@ -2018,22 +2046,22 @@
         output = (hidden + combine(mixed, select, slots, 5)).astype(jnp.bfloat16)
     (
         grad_gate_w, grad_up_w, grad_down, output, grad_tokens, grad_wq, grad_wo, grad_router,
-        grad_wk, grad_wv,
+        grad_wk, grad_wv, grad_norm1, grad_norm2, grad_query_gain, grad_key_gain,
     ) = expert_weight_grads(
-        arrived, grad_arrived, low_rows, [output, grad_tokens, grad_wq, grad_wo, grad_router],
-        grad_wkv,
+        grad_h, grad_arrived, act, [output, grad_tokens, grad_wq, grad_wo, grad_router], grad_wkv,
+        [grad_norm1, grad_norm2, grad_query_gain, grad_key_gain],
     )
     return (
         output,
         grad_tokens,
-        grad_norm1[0],
+        grad_norm1.reshape(-1),
         grad_wq,
         grad_wk.T,
         grad_wv.T,
         grad_wo,
-        grad_query_gain[0],
-        grad_key_gain[0],
-        grad_norm2[0],
+        grad_query_gain.reshape(-1),
+        grad_key_gain.reshape(-1),
+        grad_norm2.reshape(-1),
         grad_router.T,
         grad_gate_w,
         grad_up_w,

time: 500 us -> 497 us (level)
    pallas_call x1, Pallas kernels: 20.3 us -> 15.2 us  [expert_weight_grads(): pl.pallas_call(kernel, grid=(chunks,), out_shape=[jax.ShapeDtypeStruct((1...]
where the time goes in v2:
time: 497 us; the launch traced here: 489 us
  Pallas kernels  486 us (98%)
    pallas_call x1, Pallas kernels, expert_layer(): pl.pallas_call(kernel, out_shape=outs, in_specs=[whole] * 8 + [anywhere]...  164 us
    pallas_call x1, Pallas kernels, attention_backward(): pl.pallas_call(kernel, out_shape=outs, in_specs=[whole] + [anywhere] * 10...  156 us
    pallas_call x1, Pallas kernels, front(): pl.pallas_call(kernel, out_shape=kept + small, in_specs=[whole] * 15, out...  151 us
    pallas_call x1, Pallas kernels, expert_weight_grads(): pl.pallas_call(kernel, grid=(chunks,), out_shape=[jax.ShapeDtypeStruct((1...  15.2 us

profile of v2, /device:TPU:0, one launch (start us, length us, event | category | flops | bytes accessed | tf_op | source)
XLA Modules:
  0.0 489.3 jit_solution(7090766156055615371)
XLA Ops:
  0.6 0.7 fusion
  1.4 0.8 convolution_select_fusion.s_ref
  2.1 0.7 copy.35.hot_ref
  2.9 150.9 %shard_map.272 = (bf16[4,1024,512]{2,1,0:T(8,128)(2,1)}, bf16[4,512,512]{2,1,0:T(8,128)(2,1)}, bf16[2,4,128,512]{3,2,1,0:T(8,128)(2,1)}, bf16[4,512,512]{2,1,0:T...) custom-call(bf16[128,2048]{1,0:T(8,128)(2,1)} %tok_ref.3, ...), custom_call_target="tpu_custom_call" | custom-call | tf_op jit(solution)/shard_map/pallas_call | solution.py:1936
  153.7 163.8 %shard_map.273 = (bf16[2,2048,768]{2,1,0:T(8,128)(2,1)}, bf16[4,1152,512]{2,1,0:T(8,128)(2,1)}, bf16[1152,768]{1,0:T(8,128)(2,1)}, bf16[4,1152,512]{2,1,0:T(8,12...) custom-call(bf16[4,128,512]{2,1,0:T(8,128)(2,1)} %get-tuple-element., ...), custom_call_target="tpu_custom_call" | custom-call | tf_op jit(solution)/shard_map/pallas_call | solution.py:812
  317.5 156.1 %shard_map.274 = (f32[128,2048]{1,0:T(8,128)}, f32[512,512]{1,0:T(8,128)}, f32[512,512]{1,0:T(8,128)}, f32[128,512]{1,0:T(8,128)}, f32[1,128]{1,0:T(1,128)}, /*i...) custom-call(bf16[4,128,512]{2,1,0:T(8,128)(2,1)} %get-tuple-element., ...), custom_call_target="tpu_custom_call" | custom-call | tf_op jit(solution)/shard_map/pallas_call | solution.py:1436
  473.6 15.2 %shard_map.275 = (f32[1,2048,768]{2,1,0:T(8,128)}, f32[1,2048,768]{2,1,0:T(8,128)}, f32[1,768,2048]{2,1,0:T(8,128)}, bf16[128,2048]{1,0:T(8,128)(2,1)}, f32[128,...) custom-call(bf16[2,2048,768]{2,1,0:T(8,128)(2,1)} %get-tuple-element, ...), custom_call_target="tpu_custom_call" | custom-call | tf_op jit(solution)/shard_map/pallas_call | solution.py:894
  (1 shorter events, 0.0 us)

commit v3 on v2

--- a/solution.py
+++ b/solution.py
@@ -719,6 +719,14 @@
             ls2,
         )
         order = [len(sent)] + list(range(len(sent)))
+
+        def collect(k):
+            if k < len(sent):
+                c, low_col, wide = sent[k]
+                sums.result(k, summed.at[:, pl.ds(c * width + low_col, wide)])
+            else:
+                sums.result(k, pair_sum)
+
         for at, k in enumerate(order):
             give_back.wait(k)
             if k < len(sent):
@@ -739,6 +747,7 @@
                 sums.near(order[at - 1])
             if at >= 2:
                 sums.far(order[at - 2])
+                collect(order[at - 2])
             if at < chunks:
                 weight_grads(at)
         if with_mix:
@@ -747,9 +756,7 @@
         sums.near(order[-1])
         for k in order[-2:]:
             sums.far(k)
-        for k, (c, low_col, wide) in enumerate(sent):
-            sums.result(k, summed.at[:, pl.ds(c * width + low_col, wide)])
-        sums.result(len(sent), pair_sum)
+            collect(k)
 
         gate = prob_ref[...]
         grad_gate = pair_sum[:, 0:experts] + pair_sum[:, experts : 2 * experts]
@@ -1352,6 +1359,24 @@
             for k in range(1, chunks):
                 place_at = heads - mixed_at + 2 * k
                 sweeps.insert(place_at if k < mixed_at else len(sweeps), (mix_sum, k))
+
+        def settle(line, k):
+            if line is w_sum:
+                w_sum.result(k, summed)
+                wq_out[:, k * head : (k + 1) * head] = summed[...].T
+            elif line is kv_sum:
+                kv_sum.result(0, wkv_out)
+            else:
+                part_cols = pl.ds(k * width, width)
+                mix_sum.result(k, dx_sum.at[:, part_cols])
+                layer_out[:, part_cols] = (hid_ref[:, part_cols] + dx_sum[:, part_cols]).astype(
+                    jnp.bfloat16
+                )
+
+        for k in range(2):
+            wo_sum.result(k, wo_out.at[pl.ds(k * (wide // 2), wide // 2)])
+        if with_mix:
+            settle(mix_sum, 0)
         for at, (line, k) in enumerate(sweeps):
             if at == 2:
                 all_sum = vec[...]
@@ -1366,19 +1391,11 @@
                 sweeps[at - 1][0].far(sweeps[at - 1][1])
                 if at < steps + 3:
                     router_stage(at)
+                settle(*sweeps[at - 1])
         sweeps[-1][0].far(sweeps[-1][1])
+        settle(*sweeps[-1])
         for stage in range(max(1, min(len(sweeps), steps + 3)), steps + 3):
             router_stage(stage)
-        for k in range(2):
-            wo_sum.result(k, wo_out.at[pl.ds(k * (wide // 2), wide // 2)])
-        for h in range(heads):
-            w_sum.result(h, summed)
-            wq_out[:, h * head : (h + 1) * head] = summed[...].T
-        kv_sum.result(0, wkv_out)
-        if with_mix:
-            for k in range(chunks):
-                mix_sum.result(k, dx_sum.at[:, pl.ds(k * width, width)])
-            layer_out[...] = (hid_ref[...] + dx_sum[...]).astype(jnp.bfloat16)
         all_sum = vec_half[...]
         for step in range(1, data):
             vec_along(step).wait_recv()

time: 497 us -> 495 us (level)
  no operation moved by 1% of the time
where the time goes in v3:
time: 495 us; the launch traced here: 488 us
  Pallas kernels  484 us (98%)
    pallas_call x1, Pallas kernels, expert_layer(): pl.pallas_call(kernel, out_shape=outs, in_specs=[whole] * 8 + [anywhere]...  164 us
    pallas_call x1, Pallas kernels, attention_backward(): pl.pallas_call(kernel, out_shape=outs, in_specs=[whole] + [anywhere] * 10...  154 us
    pallas_call x1, Pallas kernels, front(): pl.pallas_call(kernel, out_shape=kept + small, in_specs=[whole] * 15, out...  151 us
    pallas_call x1, Pallas kernels, expert_weight_grads(): pl.pallas_call(kernel, grid=(chunks,), out_shape=[jax.ShapeDtypeStruct((1...  15.2 us

profile of v3, /device:TPU:0, one launch (start us, length us, event | category | flops | bytes accessed | tf_op | source)
XLA Modules:
  0.0 487.5 jit_solution(447851941175533695)
XLA Ops:
  0.6 0.7 fusion
  1.4 0.8 convolution_select_fusion.s_ref
  2.1 0.7 copy.35.hot_ref
  2.9 150.9 %shard_map.272 = (bf16[4,1024,512]{2,1,0:T(8,128)(2,1)}, bf16[4,512,512]{2,1,0:T(8,128)(2,1)}, bf16[2,4,128,512]{3,2,1,0:T(8,128)(2,1)}, bf16[4,512,512]{2,1,0:T...) custom-call(bf16[128,2048]{1,0:T(8,128)(2,1)} %tok_ref.3, ...), custom_call_target="tpu_custom_call" | custom-call | tf_op jit(solution)/shard_map/pallas_call | solution.py:1953
  153.7 163.7 %shard_map.273 = (bf16[2,2048,768]{2,1,0:T(8,128)(2,1)}, bf16[4,1152,512]{2,1,0:T(8,128)(2,1)}, bf16[1152,768]{1,0:T(8,128)(2,1)}, bf16[4,1152,512]{2,1,0:T(8,12...) custom-call(bf16[4,128,512]{2,1,0:T(8,128)(2,1)} %get-tuple-element., ...), custom_call_target="tpu_custom_call" | custom-call | tf_op jit(solution)/shard_map/pallas_call | solution.py:819
  317.5 154.4 %shard_map.274 = (f32[128,2048]{1,0:T(8,128)}, f32[512,512]{1,0:T(8,128)}, f32[512,512]{1,0:T(8,128)}, f32[128,512]{1,0:T(8,128)}, f32[1,128]{1,0:T(1,128)}, /*i...) custom-call(bf16[4,128,512]{2,1,0:T(8,128)(2,1)} %get-tuple-element., ...), custom_call_target="tpu_custom_call" | custom-call | tf_op jit(solution)/shard_map/pallas_call | solution.py:1453
  471.9 15.2 %shard_map.275 = (f32[1,2048,768]{2,1,0:T(8,128)}, f32[1,2048,768]{2,1,0:T(8,128)}, f32[1,768,2048]{2,1,0:T(8,128)}, bf16[128,2048]{1,0:T(8,128)(2,1)}, f32[128,...) custom-call(bf16[2,2048,768]{2,1,0:T(8,128)(2,1)} %get-tuple-element, ...), custom_call_target="tpu_custom_call" | custom-call | tf_op jit(solution)/shard_map/pallas_call | solution.py:901
  (1 shorter events, 0.0 us)

commit v4 on v3

--- a/solution.py
+++ b/solution.py
@@ -748,8 +748,10 @@
             if at >= 2:
                 sums.far(order[at - 2])
                 collect(order[at - 2])
-            if at < chunks:
-                weight_grads(at)
+            if at == 0:
+                weight_grads(0)
+            if at + 1 < chunks:
+                weight_grads(at + 1)
         if with_mix:
             mix.start(0)
             own_mix.start()

time: 495 us -> 494 us (level)
  no operation moved by 1% of the time
where the time goes in v4:
time: 494 us; the launch traced here: 487 us
  Pallas kernels  484 us (98%)
    pallas_call x1, Pallas kernels, expert_layer(): pl.pallas_call(kernel, out_shape=outs, in_specs=[whole] * 8 + [anywhere]...  163 us
    pallas_call x1, Pallas kernels, attention_backward(): pl.pallas_call(kernel, out_shape=outs, in_specs=[whole] + [anywhere] * 10...  154 us
    pallas_call x1, Pallas kernels, front(): pl.pallas_call(kernel, out_shape=kept + small, in_specs=[whole] * 15, out...  151 us
    pallas_call x1, Pallas kernels, expert_weight_grads(): pl.pallas_call(kernel, grid=(chunks,), out_shape=[jax.ShapeDtypeStruct((1...  15.2 us

profile of v4, /device:TPU:0, one launch (start us, length us, event | category | flops | bytes accessed | tf_op | source)
XLA Modules:
  0.0 487.1 jit_solution(5538097955443199715)
XLA Ops:
  0.6 0.7 fusion
  1.4 0.8 convolution_select_fusion.s_ref
  2.1 0.7 copy.35.hot_ref
  2.9 150.9 %shard_map.272 = (bf16[4,1024,512]{2,1,0:T(8,128)(2,1)}, bf16[4,512,512]{2,1,0:T(8,128)(2,1)}, bf16[2,4,128,512]{3,2,1,0:T(8,128)(2,1)}, bf16[4,512,512]{2,1,0:T...) custom-call(bf16[128,2048]{1,0:T(8,128)(2,1)} %tok_ref.3, ...), custom_call_target="tpu_custom_call" | custom-call | tf_op jit(solution)/shard_map/pallas_call | solution.py:1955
  153.7 163.3 %shard_map.273 = (bf16[2,2048,768]{2,1,0:T(8,128)(2,1)}, bf16[4,1152,512]{2,1,0:T(8,128)(2,1)}, bf16[1152,768]{1,0:T(8,128)(2,1)}, bf16[4,1152,512]{2,1,0:T(8,12...) custom-call(bf16[4,128,512]{2,1,0:T(8,128)(2,1)} %get-tuple-element., ...), custom_call_target="tpu_custom_call" | custom-call | tf_op jit(solution)/shard_map/pallas_call | solution.py:821
  317.1 154.4 %shard_map.274 = (f32[128,2048]{1,0:T(8,128)}, f32[512,512]{1,0:T(8,128)}, f32[512,512]{1,0:T(8,128)}, f32[128,512]{1,0:T(8,128)}, f32[1,128]{1,0:T(1,128)}, /*i...) custom-call(bf16[4,128,512]{2,1,0:T(8,128)(2,1)} %get-tuple-element., ...), custom_call_target="tpu_custom_call" | custom-call | tf_op jit(solution)/shard_map/pallas_call | solution.py:1455
  471.5 15.2 %shard_map.275 = (f32[1,2048,768]{2,1,0:T(8,128)}, f32[1,2048,768]{2,1,0:T(8,128)}, f32[1,768,2048]{2,1,0:T(8,128)}, bf16[128,2048]{1,0:T(8,128)(2,1)}, f32[128,...) custom-call(bf16[2,2048,768]{2,1,0:T(8,128)(2,1)} %get-tuple-element, ...), custom_call_target="tpu_custom_call" | custom-call | tf_op jit(solution)/shard_map/pallas_call | solution.py:903
  (1 shorter events, 0.0 us)
